TPU v7x, 768 devices: a whole 4x8x12 slice. The times are simulated.
768 devices in a mesh: gx: 3 (over z_lo), gy: 16 (over y, core), gz: 16 (over z_hi, x).
Axes of the slice: x: 4, y: 8, z: 12 (z_hi: 4, z_lo: 3; z = z_hi * 3 + z_lo), core: 2. Of those that a mesh axis runs over, the one named last changes fastest.
Arguments:
- positions: float32 [3, 16, 16, 3, 18], P('gx', 'gy', 'gz'), may hold values from 0 to 7, as said below
- species: int32 [3, 16, 16, 18], P('gx', 'gy', 'gz'), may hold values from 0 to 88
- send_rows: int32 [3, 16, 16, 18], P('gx', 'gy', 'gz'), may hold values from 0 to 17, as said below
- neighbours: int32 [3, 16, 16, 56, 18], P('gx', 'gy', 'gz'), may hold values from -1 to 503, as said below
- embedding: float32 [89, 128], replicated, may hold values from -6 to 6
- self_energy: float32 [89], replicated, may hold values from -6 to 6
- source_weight: float32 [2, 128, 128], replicated, may hold values from -0.5 to 0.5
- radial_in: float32 [2, 8, 64], replicated, may hold values from -6 to 6
- radial_out: float32 [2, 64, 384], replicated, may hold values from -0.75 to 0.75
- mix_weight: float32 [2, 384, 128], replicated, may hold values from -0.3125 to 0.3125
- read_one: float32 [128], replicated, may hold values from -0.5 to 0.5
- read_hidden: float32 [128, 16], replicated, may hold values from -0.5 to 0.5
- read_two: float32 [16], replicated, may hold values from -1.5 to 1.5
Outputs:
- atom_energy: float32 [3, 16, 16, 18], P('gx', 'gy', 'gz')
- forces: float32 [3, 16, 16, 3, 18], P('gx', 'gy', 'gz')
Inputs may be any that keep to these rules, and one draw needn't show every extreme that they name: `positions`: atom a lies within 0.4 of each coordinate of its lattice cell's centre 2.5 (a // 6 + 0.5, a // 2 % 3 + 0.5, a % 2 + 0.5). `send_rows`: the 18 entries of a domain are a permutation of its 18 atoms (with 3 = 3 and 2 = 2 every lattice cell lies in the outer two layers). `neighbours`: entries are rows of the domain's row table of 504 rows; -1 marks an empty slot. No entry names block b = 13 or a domain beyond the ends of gz; every named row lies within 8.5 of the atom, and every atom within 6 of an atom either is named in one of its slots or has been left out of its list.
All inputs are finite; a program needn't handle non-finite values.
Results may differ from a plain program's by a relative error of at most 0.0003.
Values sent between devices are 32-bit elements; how exact they have to be, the bound alone decides.
A program may use at most 32 MiB of HBM per device.

v0:
```python
import functools
import math

import jax
import jax.numpy as jnp
from jax import lax
from jax.experimental import pallas as pl
from jax.experimental.pallas import tpu as pltpu
from jax.sharding import PartitionSpec as P

F32 = jnp.float32
BF16 = jnp.bfloat16
HIGHEST = lax.Precision.HIGHEST
MESH = pl.DeviceIdType.MESH
CUTOFF = 6.0
BOX = (7.5, 7.5, 5.0)
ATOMS = 18
SLOTS = 56
CHANNELS = 128
HIDDEN = 64
ORDERS = 8
ROWS = 24
TABLE = 28 * ROWS
EDGES = 1024
TILES = 8
CHUNK = 16
OWN = 13
OFFSETS = tuple((b // 9 - 1, b // 3 % 3 - 1, b % 3 - 1) for b in range(27))
OTHERS = tuple(b for b in range(27) if b != OWN)
NN = ((1,), (0,))
NT = ((1,), (1,))
TN = ((0,), (0,))


def dot(left, right, dims, precision=None):
    return lax.dot_general(
        left, right, (dims, ((), ())), precision=precision, preferred_element_type=F32
    )


def halves(value):
    high = value.astype(BF16).astype(F32)
    return high, value - high


def dot_split(left, right, dims):
    left_high, left_low = halves(left)
    right_high, right_low = halves(right)
    left_high = left_high.astype(BF16)
    right_high = right_high.astype(BF16)
    return (
        dot(left_high, right_high, dims)
        + dot(left_high, right_low.astype(BF16), dims)
        + dot(left_low.astype(BF16), right_high, dims)
    )


def iota(shape, dim):
    return lax.broadcasted_iota(jnp.int32, shape, dim)


def over(value, divisor):
    return (value * (65536 // divisor + 1)) >> 16


def lanes(index):
    return pl.ds(pl.multiple_of(index * 128, 128), 128)


def column(row, rows):
    return jnp.transpose(jnp.broadcast_to(row, (128, 128)))[0:rows]


def packed(values):
    row = values[0:1]
    for c in range(1, 4):
        row = row + pltpu.roll(values[c : c + 1], 32 * c, 1)
    return row


def unrolled(values, c):
    return values if c == 0 else pltpu.roll(values, 128 - 32 * c, 1)


def kernel(
    pos_ref,
    species_ref,
    send_ref,
    nbr_ref,
    emb_ref,
    self_ref,
    source_ref,
    rin_ref,
    rout_ref,
    mix_ref,
    read_one_ref,
    read_hidden_ref,
    read_two_ref,
    energy_ref,
    force_ref,
    stage,
    slots,
    table_emb,
    packet,
    arrived,
    leaving,
    returned,
    feat,
    feat_grad,
    feat_back,
    onehot,
    ghot,
    bhot,
    geo,
    basis_ref,
    dbasis_ref,
    harm,
    harm_grad,
    r_grad,
    radial,
    dsilu,
    source,
    source_grad,
    acc,
    expanded,
    grad_high,
    grad_low,
    sent,
    received,
):
    me = (lax.axis_index("gx"), lax.axis_index("gy"), lax.axis_index("gz"))
    extent = (3, 16, 16)

    def device(offset):
        return tuple(lax.rem(m + (o + n), n) for m, o, n in zip(me, offset, extent))

    def minus(offset):
        return tuple(-o for o in offset)

    barrier = pltpu.get_barrier_semaphore()
    for b in OTHERS:
        pl.semaphore_signal(barrier, inc=1, device_id=device(OFFSETS[b]), device_id_type=MESH)

    def remote(phase, index, src, dst, offset):
        return pltpu.make_async_remote_copy(
            src_ref=src,
            dst_ref=dst,
            send_sem=sent.at[phase, index],
            recv_sem=received.at[phase, index],
            device_id=device(offset),
            device_id_type=MESH,
        )

    stage[...] = jnp.zeros_like(stage)
    stage[0:3, 0:ATOMS] = pos_ref[0, 0, 0]
    stage[3:4, 0:ATOMS] = species_ref[0, 0].astype(F32)
    stage[8:9, 0:ATOMS] = send_ref[0, 0].astype(F32)
    lane = iota((128, 128), 1)
    row = iota((128, 128), 0)
    send_row = jnp.where(lane[0:1] < ATOMS, stage[8:9], -5.0)
    own = stage[0:8]
    to_send = (row.astype(F32) == send_row).astype(F32)
    own_send = dot(own, to_send, NN, HIGHEST)
    packet[0] = packed(own_send)
    arrived[OWN] = packed(own)
    arrived[27:32] = jnp.zeros((5, 1, 128), F32)
    pl.semaphore_wait(barrier, 26)
    first = [
        remote(0, b, packet.at[0], arrived.at[b], minus(OFFSETS[b])) for b in OTHERS
    ]
    for copy in first:
        copy.start()

    send_col = column(send_row, 128)
    lane_atom = jnp.where(lane < 7 * ATOMS, lane - ATOMS * over(lane, ATOMS), -7)
    select = (send_col[0:ROWS] == lane_atom[0:ROWS].astype(F32)).astype(F32)
    select_wide = jnp.concatenate([select, select], axis=1).astype(BF16)
    select_deep = jnp.concatenate([select, select], axis=0).astype(BF16)
    unsend = (send_col == lane.astype(F32)).astype(F32)
    spread = (row == lane_atom).astype(F32)
    centre = dot(own, spread, NN, HIGHEST)

    slots[...] = jnp.zeros_like(slots)
    slots[:, 0:ATOMS] = (nbr_ref[0, 0, 0] + 1).astype(F32)
    named = slots[0:8]
    for j in range(1, 7):
        named = named + pltpu.roll(slots[8 * j : 8 * j + 8], ATOMS * j, 1)
    named = named.astype(jnp.int32) - 1
    outer = jnp.maximum(named - ATOMS, 0)
    block = jnp.where(named < 0, -1, jnp.where(named < ATOMS, OWN, over(outer, ATOMS)))
    member = jnp.where(named < ATOMS, named, outer - ATOMS * over(outer, ATOMS))
    usable = (named >= 0).astype(F32)

    table_row = iota((TABLE, 128), 0)
    table_block = over(table_row, ROWS)
    table_member = table_row - ROWS * table_block
    label = jnp.where(
        (table_member < ATOMS) & (table_block < 27),
        ATOMS + ATOMS * table_block + table_member,
        -2,
    )
    label = jnp.concatenate(
        [label[0 : OWN * ROWS], send_col[0:ROWS].astype(jnp.int32), label[(OWN + 1) * ROWS :]],
        axis=0,
    )
    for k in range(TILES):
        tile = slice(128 * k, 128 * k + 128)
        onehot[:, tile] = (label == named[k : k + 1]).astype(F32).astype(BF16)
        ghot[:, tile] = (row == member[k : k + 1]).astype(F32).astype(BF16)
        bhot[k] = (row[0:32] == block[k : k + 1]).astype(F32)

    table_emb[...] = jnp.zeros_like(table_emb)
    table_emb[0:89] = emb_ref[...]
    table_emb[128:129, 0:89] = self_ref[...]
    embedding = table_emb[0:128]
    species_col = column(own_send[3:4], ROWS)
    own_hot = (
        (species_col == lane[0:ROWS].astype(F32)) & (row[0:ROWS] < ATOMS)
    ).astype(F32)
    h_zero = dot(own_hot, embedding, NN, HIGHEST)
    isolated = jnp.sum(own_hot * table_emb[128:129], axis=1, keepdims=True)
    emb_source = dot_split(jnp.transpose(source_ref[0]), embedding, NT)
    emb_source = jnp.concatenate(halves(emb_source), axis=0).astype(BF16)

    rin_high, rin_low = halves(jnp.concatenate([rin_ref[0], rin_ref[1]], axis=1))
    rin_wide = jnp.concatenate(
        [rin_high, rin_high, rin_low, jnp.zeros((104, 128), F32)], axis=0
    )
    rin_wide = jnp.transpose(rin_wide)[:, 0:32].astype(BF16)
    rin_back = []
    rout_wide = []
    rout_back = []
    for t in range(2):
        high, low = halves(rout_ref[t])
        rout_wide.append(
            jnp.transpose(jnp.concatenate([high, high, low, low], axis=0)).astype(BF16)
        )
        rout_back.append(jnp.concatenate([high, low], axis=0).astype(BF16))
        high, low = halves(rin_ref[t])
        rin_back.append(jnp.concatenate([high, low], axis=0).astype(BF16))

    for copy in first:
        copy.wait_recv()
    lane_part = over(lane[0:32], 32)
    domain = row[0:32]
    third = over(domain, 3)
    shift = jnp.where(
        lane_part == 0,
        (over(domain, 9) - 1).astype(F32) * BOX[0],
        jnp.where(
            lane_part == 1,
            (third - 3 * over(domain, 9) - 1).astype(F32) * BOX[1],
            jnp.where(lane_part == 2, (domain - 3 * third - 1).astype(F32) * BOX[2], 0.0),
        ),
    )
    nearby = arrived[...].reshape(32, 128) + shift
    nearby = jnp.concatenate([unrolled(nearby, c) for c in range(4)], axis=0)
    high, low = halves(nearby)
    middle, low = halves(low)
    nearby = jnp.concatenate([high, middle, low], axis=0).astype(BF16)
    by_block = dot(nearby, ghot[...], NN)
    by_block = by_block[0:128] + by_block[128:256] + by_block[256:384]
    for k in range(TILES):
        tile = slice(128 * k, 128 * k + 128)
        for c in range(4):
            geo[c, k : k + 1, :] = jnp.sum(
                by_block[32 * c : 32 * c + 32, tile] * bhot[k], axis=0, keepdims=True
            )

    dx = geo[0] - centre[0:1]
    dy = geo[1] - centre[1:2]
    dz = geo[2] - centre[2:3]
    distance = jnp.sqrt(dx * dx + dy * dy + dz * dz + 0.25)
    inverse = 1.0 / distance
    nx = dx * inverse
    ny = dy * inverse
    nz = dz * inverse
    scaled = jnp.minimum(distance * (1.0 / CUTOFF), 1.0)
    square = scaled * scaled
    fifth = square * square * scaled
    sixth = fifth * scaled
    seventh = sixth * scaled
    envelope = 1.0 - 28.0 * sixth + 48.0 * seventh - 21.0 * seventh * scaled
    envelope_grad = (-168.0 * fifth + 336.0 * sixth - 168.0 * seventh) * (1.0 / CUTOFF)
    weight = math.sqrt(2.0 / CUTOFF) * inverse * usable
    weight_grad = weight * (envelope_grad - envelope * inverse)
    weight = weight * envelope
    angle = distance * (math.pi / CUTOFF)
    sine_one = jnp.sin(angle)
    cosine_one = jnp.cos(angle)
    sine, cosine = sine_one, cosine_one
    sine_last, cosine_last = jnp.zeros_like(angle), jnp.ones_like(angle)
    for m in range(ORDERS):
        basis_ref[:, m, :] = weight * sine
        dbasis_ref[:, m, :] = weight_grad * sine + weight * cosine * ((m + 1) * math.pi / CUTOFF)
        sine, sine_last = 2.0 * cosine_one * sine - sine_last, sine
        cosine, cosine_last = 2.0 * cosine_one * cosine - cosine_last, cosine
    r3, r5, r15 = math.sqrt(3.0), math.sqrt(5.0), math.sqrt(15.0)
    for m, value in enumerate(
        (
            r3 * nx,
            r3 * ny,
            r3 * nz,
            r15 * nx * ny,
            r15 * ny * nz,
            0.5 * r5 * (3.0 * nz * nz - 1.0),
            r15 * nx * nz,
            0.5 * r15 * (nx * nx - ny * ny),
        )
    ):
        harm[:, m, :] = value

    basis = jnp.concatenate([basis_ref[k] for k in range(TILES)], axis=1)
    high, low = halves(basis)
    basis = jnp.concatenate([high, low, high, jnp.zeros_like(high)], axis=0).astype(BF16)
    pre = dot(rin_wide, basis, NN)
    gate = 1.0 / (1.0 + jnp.exp(-pre))
    hidden = pre * gate
    dsilu[...] = gate * (1.0 + pre * (1.0 - gate))
    hidden_high, hidden_low = halves(hidden)

    def radial_layer(t):
        rows = slice(HIDDEN * t, HIDDEN * t + HIDDEN)
        deep = jnp.concatenate(
            [hidden_high[rows], hidden_low[rows], hidden_high[rows], hidden_low[rows]], axis=0
        )
        radial[t] = dot(rout_wide[t], deep.astype(BF16), NN)

    def gather_sum(t):
        def chunk(ci, carry):
            c0 = pl.multiple_of(ci * CHUNK, CHUNK)
            rows = [pl.ds(pl.multiple_of(128 * q + c0, CHUNK), CHUNK) for q in range(3)]
            sums = [None] * 9
            for k in range(TILES):
                tile = slice(128 * k, 128 * k + 128)
                src = source[t, rows[0], tile]
                terms = [radial[t, rows[q], tile] * src for q in range(3)]
                ys = harm[k]
                parts = [terms[0]]
                parts += [terms[1] * ys[m : m + 1] for m in range(3)]
                parts += [terms[2] * ys[m : m + 1] for m in range(3, 8)]
                sums = [p if s is None else s + p for s, p in zip(sums, parts)]
            for i in range(9):
                acc[i, rows[0], :] = sums[i]
            return carry

        lax.fori_loop(0, CHANNELS // CHUNK, chunk, 0)

    def interaction(t, feats):
        gather_sum(t)
        wide = acc[...].reshape(9 * 128, 128)
        wide = jnp.concatenate(halves(wide), axis=1).astype(BF16)
        moments = 0.25 * dot(select_wide, wide, NT)
        parts = [moments[:, 128 * i : 128 * i + 128] for i in range(9)]
        vector = parts[1] * parts[1] + parts[2] * parts[2] + parts[3] * parts[3]
        tensor = parts[4] * parts[4]
        for i in range(5, 9):
            tensor = tensor + parts[i] * parts[i]
        invariants = jnp.concatenate([parts[0], vector, tensor], axis=1)
        return feats + dot_split(invariants, mix_ref[t], NN), parts

    def interaction_back(t, grad, parts, with_source):
        inv_grad = dot_split(grad, mix_ref[t], NT)
        grads = [0.25 * inv_grad[:, 0:128]]
        grads += [0.5 * inv_grad[:, 128:256] * parts[i] for i in range(1, 4)]
        grads += [0.5 * inv_grad[:, 256:384] * parts[i] for i in range(4, 9)]
        deep = jnp.concatenate(grads, axis=1)
        deep = jnp.concatenate(halves(deep), axis=0).astype(BF16)
        expanded[...] = dot(deep, select_deep, TN).reshape(9, 128, 128)

        def tile_back(k, carry):
            tile = lanes(k)
            ys = harm[k]
            sums = [jnp.zeros((8, 128), F32)] * 8
            for ci in range(CHANNELS // CHUNK):
                rows = [slice(128 * q + CHUNK * ci, 128 * q + CHUNK * ci + CHUNK) for q in range(3)]
                src = source[t, rows[0], tile]
                rads = [radial[t, rows[q], tile] for q in range(3)]
                wide = [expanded[i, rows[0], :] for i in range(9)]
                pulls = [wide[0], wide[1] * ys[0:1], wide[4] * ys[3:4]]
                for m in range(1, 3):
                    pulls[1] = pulls[1] + wide[1 + m] * ys[m : m + 1]
                for m in range(4, 8):
                    pulls[2] = pulls[2] + wide[1 + m] * ys[m : m + 1]
                if with_source:
                    high, low = halves(
                        rads[0] * pulls[0] + rads[1] * pulls[1] + rads[2] * pulls[2]
                    )
                    source_grad[rows[0], tile] = high.astype(BF16)
                    source_grad[rows[1], tile] = low.astype(BF16)
                for q in range(3):
                    high, low = halves(src * pulls[q])
                    grad_high[rows[q], tile] = high.astype(BF16)
                    grad_low[rows[q], tile] = low.astype(BF16)
                for m in range(8):
                    value = wide[1 + m] * (rads[1 if m < 3 else 2] * src)
                    sums[m] = sums[m] + (value[0:8] + value[8:16])
            tops = [jnp.sum(s, axis=0, keepdims=True) for s in sums]
            harm_grad[t, k] = jnp.concatenate(tops, axis=0)
            return carry

        lax.fori_loop(0, TILES, tile_back, 0)

    def radial_back(t):
        rows = slice(HIDDEN * t, HIDDEN * t + HIDDEN)
        both = dot(rout_back[t], grad_high[...], NN)
        grad = both[0:HIDDEN] + both[HIDDEN : 2 * HIDDEN]
        grad = grad + dot(rout_back[t][0:HIDDEN], grad_low[...], NN)
        high, low = halves(grad * dsilu[rows])
        both = dot(rin_back[t], high.astype(BF16), NN)
        grad = both[0:ORDERS] + both[ORDERS : 2 * ORDERS]
        grad = grad + dot(rin_back[t][0:ORDERS], low.astype(BF16), NN)
        for k in range(TILES):
            r_grad[t, k : k + 1, :] = jnp.sum(
                grad[:, 128 * k : 128 * k + 128] * dbasis_ref[k], axis=0, keepdims=True
            )

    radial_layer(0)
    element = geo[3]
    for k in range(TILES):
        tile = slice(128 * k, 128 * k + 128)
        hot = (row.astype(F32) == element[k : k + 1]).astype(F32).astype(BF16)
        both = dot(emb_source, hot, NN)
        source[0, :, tile] = both[0:128] + both[128:256]
    h_one, parts_one = interaction(0, h_zero)

    feat[OWN] = dot_split(h_one, source_ref[1], NN)
    feat[27] = jnp.zeros((ROWS, 128), F32)
    second = [
        remote(1, b, feat.at[OWN], feat.at[b], minus(OFFSETS[b])) for b in OTHERS
    ]
    for copy in second:
        copy.start()
    radial_layer(1)
    for copy in second:
        copy.wait_recv()

    table = jnp.transpose(feat[...].reshape(TABLE, 128))
    table = jnp.concatenate(halves(table), axis=0).astype(BF16)
    both = dot(table, onehot[...], NN)
    source[1] = both[0:128] + both[128:256]
    h_two, parts_two = interaction(1, h_one)
    inner = dot_split(h_two, read_hidden_ref[...], NN)
    gate = 1.0 / (1.0 + jnp.exp(-inner))
    learned = jnp.sum(h_one * read_one_ref[...], axis=1, keepdims=True) + jnp.sum(
        inner * gate * read_two_ref[...], axis=1, keepdims=True
    )
    energy = jnp.sum((isolated + learned) * unsend[0:ROWS], axis=0, keepdims=True)
    energy_ref[0, 0] = energy[:, 0:ATOMS]
    inner_grad = gate * (1.0 + inner * (1.0 - gate)) * read_two_ref[...]
    grad_two = dot_split(inner_grad, read_hidden_ref[...], NT)
    interaction_back(1, grad_two, parts_two, True)

    both = dot(onehot[...], source_grad[...], NT)
    feat_grad[...] = (both[:, 0:128] + both[:, 128:256]).reshape(28, ROWS, 128)
    third_copies = [
        remote(2, b, feat_grad.at[b], feat_back.at[b], OFFSETS[b]) for b in OTHERS
    ]
    for copy in third_copies:
        copy.start()
    radial_back(1)
    for copy in third_copies:
        copy.wait_recv()
    total = feat_grad[OWN]
    for b in OTHERS:
        total = total + feat_back[b]
    grad_one = grad_two + read_one_ref[...] + dot_split(total, source_ref[1], NT)

    interaction_back(0, grad_one, parts_one, False)
    radial_back(0)

    pulls = [harm_grad[0, :, m, :] + harm_grad[1, :, m, :] for m in range(8)]
    along = r_grad[0] + r_grad[1]
    gx = r3 * pulls[0] + r15 * (ny * pulls[3] + nz * pulls[6] + nx * pulls[7])
    gy = r3 * pulls[1] + r15 * (nx * pulls[3] + nz * pulls[4] - ny * pulls[7])
    gz = r3 * pulls[2] + r15 * (ny * pulls[4] + nx * pulls[6]) + 3.0 * r5 * nz * pulls[5]
    radially = along - (nx * gx + ny * gy + nz * gz) * inverse
    pulls = [radially * n + g * inverse for n, g in ((nx, gx), (ny, gy), (nz, gz))]
    highs = []
    for k in range(TILES):
        blocks = jnp.concatenate([bhot[k] * p[k : k + 1] for p in pulls], axis=0)
        highs.append(jnp.concatenate(halves(blocks), axis=0))
    blocks = jnp.concatenate(highs, axis=1).astype(BF16)
    both = dot(blocks, ghot[...], NT)
    both = both[0:96] + both[96:192]
    rows = both[0:32]
    for c in range(1, 3):
        rows = rows + pltpu.roll(both[32 * c : 32 * c + 32], 32 * c, 1)
    for b in range(27):
        leaving[b] = rows[b : b + 1]
    fourth = [
        remote(3, b, leaving.at[b], returned.at[b], OFFSETS[b]) for b in OTHERS
    ]
    for copy in fourth:
        copy.start()
    sums = [jnp.sum(p, axis=0, keepdims=True) for p in pulls] + [jnp.zeros((5, 128), F32)]
    force = dot(jnp.concatenate(sums, axis=0), spread, NT, HIGHEST)
    own_row = rows[OWN : OWN + 1]
    force = force - jnp.concatenate([unrolled(own_row, c) for c in range(3)] + [sums[3]], axis=0)
    for copy in fourth:
        copy.wait_recv()
    back = returned[OTHERS[0]]
    for b in OTHERS[1:]:
        back = back + returned[b]
    back = jnp.concatenate([unrolled(back, c) for c in range(3)] + [sums[3]], axis=0)
    force = force - dot(back, unsend, NN, HIGHEST)
    force_ref[0, 0, 0] = force[0:3, 0:ATOMS]
    for copy in first + second + third_copies + fourth:
        copy.wait_send()


def per_device(
    positions,
    species,
    send_rows,
    neighbours,
    embedding,
    self_energy,
    source_weight,
    radial_in,
    radial_out,
    mix_weight,
    read_one,
    read_hidden,
    read_two,
):
    vmem = pl.BlockSpec(memory_space=pltpu.VMEM)
    energy, forces = pl.pallas_call(
        kernel,
        out_shape=(
            jax.ShapeDtypeStruct((1, 1, 1, ATOMS), F32),
            jax.ShapeDtypeStruct((1, 1, 1, 3, ATOMS), F32),
        ),
        in_specs=[vmem] * 13,
        out_specs=(vmem, vmem),
        scratch_shapes=[
            pltpu.VMEM((16, 128), F32),
            pltpu.VMEM((SLOTS, 128), F32),
            pltpu.VMEM((136, 128), F32),
            pltpu.VMEM((1, 1, 128), F32),
            pltpu.VMEM((32, 1, 128), F32),
            pltpu.VMEM((27, 1, 128), F32),
            pltpu.VMEM((27, 1, 128), F32),
            pltpu.VMEM((28, ROWS, 128), F32),
            pltpu.VMEM((28, ROWS, 128), F32),
            pltpu.VMEM((27, ROWS, 128), F32),
            pltpu.VMEM((TABLE, EDGES), BF16),
            pltpu.VMEM((128, EDGES), BF16),
            pltpu.VMEM((TILES, 32, 128), F32),
            pltpu.VMEM((4, 8, 128), F32),
            pltpu.VMEM((TILES, ORDERS, 128), F32),
            pltpu.VMEM((TILES, ORDERS, 128), F32),
            pltpu.VMEM((TILES, 8, 128), F32),
            pltpu.VMEM((2, TILES, 8, 128), F32),
            pltpu.VMEM((2, TILES, 128), F32),
            pltpu.VMEM((2, 384, EDGES), F32),
            pltpu.VMEM((128, EDGES), F32),
            pltpu.VMEM((2, 128, EDGES), F32),
            pltpu.VMEM((256, EDGES), BF16),
            pltpu.VMEM((9, 128, 128), F32),
            pltpu.VMEM((9, 128, 128), F32),
            pltpu.VMEM((384, EDGES), BF16),
            pltpu.VMEM((384, EDGES), BF16),
            pltpu.SemaphoreType.DMA((4, 27)),
            pltpu.SemaphoreType.DMA((4, 27)),
        ],
        compiler_params=pltpu.CompilerParams(
            collective_id=0, has_side_effects=True, vmem_limit_bytes=48 * 1024 * 1024
        ),
        name="energy_and_forces",
    )(
        positions,
        species,
        send_rows,
        neighbours,
        embedding,
        self_energy[None],
        source_weight,
        radial_in,
        radial_out,
        mix_weight,
        read_one[None],
        read_hidden,
        read_two[None],
    )
    return energy, forces


def solution(mesh):
    return jax.shard_map(
        per_device,
        mesh=mesh,
        in_specs=(
            P("gx", "gy", "gz", None, None),
            P("gx", "gy", "gz", None),
            P("gx", "gy", "gz", None),
            P("gx", "gy", "gz", None, None),
            P(),
            P(),
            P(),
            P(),
            P(),
            P(),
            P(),
            P(),
            P(),
        ),
        out_specs=(P("gx", "gy", "gz", None), P("gx", "gy", "gz", None, None)),
        check_vma=False,
    )
```

profile of v0, /device:TPU:1, one launch (start us, length us, event | category | flops | bytes accessed | tf_op | source)
XLA Modules:
  0.0 76.0 jit_solution(6577273215242450392)
XLA Ops:
  0.6 0.0 copy-start.10
  0.6 0.0 copy-start.11
  0.6 0.7 copy.15.pos_ref
  1.3 0.0 copy-done.10
  1.3 0.0 copy-start.3
  1.3 0.1 copy.16.nbr_ref
  1.4 0.0 copy-done.11
  1.4 0.0 copy-start.4
  1.4 0.0 copy-start.5
  1.5 0.0 copy-start.6
  1.5 0.0 copy-start.7
  1.5 0.0 copy-start.8
  1.5 0.0 copy-start.9
  1.5 0.1 copy.17.read_hidden_ref
  1.6 0.5 copy-done.3
  2.1 0.0 copy-done.4
  2.1 0.0 copy-done.5
  2.2 0.0 copy-done.6
  2.2 0.0 copy-done.7
  2.2 0.0 copy-done.8
  2.2 0.0 copy-done.9
  2.2 0.0 copy-start
  2.2 1.0 %copy-done = f32[2,384,128]{2,1,0:T(8,128)S(1)} copy-done((f32[2,384,128]{2,1,0:T(8,128)S(1)}, f32[2,384,128]{2,1,0:T(8,128)}, u32[]{:S(2)}) %copy-start) | copy-done | bytes 393240
  3.2 0.0 copy-start.1
  3.2 0.9 %copy-done.1 = f32[2,64,384]{2,1,0:T(8,128)S(1)} copy-done((f32[2,64,384]{2,1,0:T(8,128)S(1)}, f32[2,64,384]{2,1,0:T(8,128)}, u32[]{:S(2)}) %copy-start.1) | copy-done | bytes 196632
  4.1 0.0 copy-start.2
  4.1 0.9 %copy-done.2 = f32[2,128,128]{2,1,0:T(8,128)S(1)} copy-done((f32[2,128,128]{2,1,0:T(8,128)S(1)}, f32[2,128,128]{2,1,0:T(8,128)}, u32[]{:S(2)}) %copy-start.2) | copy-done | bytes 131096
  5.0 69.9 %energy_and_forces.1 = (f32[1,1,1,18]{3,2,1,0:T(1,128)S(1)}, f32[1,1,1,3,18]{4,3,2,1,0:T(4,128)S(1)}) custom-call(f32[1,1,1,3,18]{4,3,2,1,0:T(4,128)S(1)} %copy.15.pos_ref, s32[1,1,1,18]{3,2,1,0:T(1,128)S(1)} %copy-done.5, s32[1,1,1,18]{3,2,1,0:T(1,128)S(1)} %copy-done.6, s32[1,1,1,56,18]{4,3,2,1,0:T(8,128)S(1)} %copy.16.nbr_ref, f32[89,128]{1,0:T(8,128)S(1)} %copy-done.3, ...), custom_call_target="tpu_custom_call" | custom-call | tf_op jit(solution)/shard_map/energy_and_forces/pallas_call | solution.py:528
  74.9 0.6 copy.18
  75.5 0.5 copy.20
Async XLA Ops:
  0.6 0.7 copy-start.10
  0.6 0.8 %copy-start.11 = (f32[128,16]{0,1:T(8,128)S(1)}, f32[128,16]{0,1:T(8,128)}, u32[]{:S(2)}) copy-start(f32[128,16]{0,1:T(8,128)} %param.24) | copy-start | bytes 24580
  1.3 0.8 %copy-start.3 = (f32[89,128]{1,0:T(8,128)S(1)}, f32[89,128]{1,0:T(8,128)}, u32[]{:S(2)}) copy-start(f32[89,128]{1,0:T(8,128)} %emb_ref.1) | copy-start | bytes 136708
  1.4 0.7 copy-start.4
  1.4 0.7 copy-start.5
  1.5 0.7 copy-start.6
  1.5 0.7 copy-start.7
  1.5 0.7 copy-start.8
  1.5 0.7 copy-start.9
  2.2 1.0 %copy-start = (f32[2,384,128]{2,1,0:T(8,128)S(1)}, f32[2,384,128]{2,1,0:T(8,128)}, u32[]{:S(2)}) copy-start(f32[2,384,128]{2,1,0:T(8,128)} %mix_ref.1) | copy-start | bytes 1179652
  3.2 0.9 %copy-start.1 = (f32[2,64,384]{2,1,0:T(8,128)S(1)}, f32[2,64,384]{2,1,0:T(8,128)}, u32[]{:S(2)}) copy-start(f32[2,64,384]{2,1,0:T(8,128)} %rout_ref.1) | copy-start | bytes 589828
  4.1 0.9 %copy-start.2 = (f32[2,128,128]{2,1,0:T(8,128)S(1)}, f32[2,128,128]{2,1,0:T(8,128)}, u32[]{:S(2)}) copy-start(f32[2,128,128]{2,1,0:T(8,128)} %source_ref.1) | copy-start | bytes 393220
where the time goes:
time: 76.3 us; the launch traced here: 76 us
  Pallas kernels  69.9 us (92%)
  local copies, waits for them, and re-layouts  5.37 us (7%)
    pallas_call x1, Pallas kernels, per_device(): pl.pallas_call(kernel, out_shape=(jax.ShapeDtypeStruct((1, 1, 1, ATOMS),...  69.9 us
    unnamed x28, local copies, waits for them, and re-layouts  4.8 us

commit v1 on v0

--- a/solution.py
+++ b/solution.py
@@ -26,7 +26,12 @@
 CHUNK = 16
 OWN = 13
 OFFSETS = tuple((b // 9 - 1, b // 3 % 3 - 1, b % 3 - 1) for b in range(27))
-OTHERS = tuple(b for b in range(27) if b != OWN)
+OTHERS = tuple(
+    sorted(
+        (b for b in range(27) if b != OWN),
+        key=lambda b: -sum(abs(o) * w for o, w in zip(OFFSETS[b], (2, 1, 4))),
+    )
+)
 NN = ((1,), (0,))
 NT = ((1,), (1,))
 TN = ((0,), (0,))
@@ -36,6 +41,14 @@
     return lax.dot_general(
         left, right, (dims, ((), ())), precision=precision, preferred_element_type=F32
     )
+
+
+def pick(value, selector, dims):
+    high, low = halves(value)
+    middle, low = halves(low)
+    parts = jnp.concatenate([high, middle, low, jnp.zeros_like(low)], axis=0).astype(BF16)
+    parts = dot(parts, selector.astype(BF16), dims)
+    return (parts[0:8] + parts[8:16]) + parts[16:24]
 
 
 def halves(value):
@@ -87,17 +100,22 @@
     species_ref,
     send_ref,
     nbr_ref,
-    emb_ref,
+    emb_hbm,
     self_ref,
-    source_ref,
-    rin_ref,
-    rout_ref,
-    mix_ref,
+    source_hbm,
+    rin_hbm,
+    rout_hbm,
+    mix_hbm,
     read_one_ref,
     read_hidden_ref,
     read_two_ref,
     energy_ref,
     force_ref,
+    emb_ref,
+    source_ref,
+    rin_ref,
+    rout_ref,
+    mix_ref,
     stage,
     slots,
     table_emb,
@@ -105,7 +123,9 @@
     arrived,
     leaving,
     returned,
+    mine,
     feat,
+    table,
     feat_grad,
     feat_back,
     onehot,
@@ -115,18 +135,19 @@
     basis_ref,
     dbasis_ref,
     harm,
-    harm_grad,
-    r_grad,
+    edge_grad,
     radial,
+    slope,
+    term,
     dsilu,
+    later,
     source,
     source_grad,
     acc,
     expanded,
-    grad_high,
-    grad_low,
     sent,
     received,
+    loaded,
 ):
     me = (lax.axis_index("gx"), lax.axis_index("gy"), lax.axis_index("gz"))
     extent = (3, 16, 16)
@@ -137,9 +158,23 @@
     def minus(offset):
         return tuple(-o for o in offset)
 
+    inputs = [
+        pltpu.make_async_copy(src, dst, loaded.at[i])
+        for i, (src, dst) in enumerate(
+            (
+                (emb_hbm, emb_ref),
+                (source_hbm, source_ref),
+                (rin_hbm, rin_ref),
+                (rout_hbm, rout_ref),
+                (mix_hbm, mix_ref),
+            )
+        )
+    ]
     barrier = pltpu.get_barrier_semaphore()
     for b in OTHERS:
         pl.semaphore_signal(barrier, inc=1, device_id=device(OFFSETS[b]), device_id_type=MESH)
+    for copy in inputs:
+        copy.start()
 
     def remote(phase, index, src, dst, offset):
         return pltpu.make_async_remote_copy(
@@ -152,7 +187,8 @@
         )
 
     stage[...] = jnp.zeros_like(stage)
-    stage[0:3, 0:ATOMS] = pos_ref[0, 0, 0]
+    for c in range(3):
+        stage[c : c + 1, 0:ATOMS] = pos_ref[0, 0, c]
     stage[3:4, 0:ATOMS] = species_ref[0, 0].astype(F32)
     stage[8:9, 0:ATOMS] = send_ref[0, 0].astype(F32)
     lane = iota((128, 128), 1)
@@ -160,7 +196,7 @@
     send_row = jnp.where(lane[0:1] < ATOMS, stage[8:9], -5.0)
     own = stage[0:8]
     to_send = (row.astype(F32) == send_row).astype(F32)
-    own_send = dot(own, to_send, NN, HIGHEST)
+    own_send = pick(own, to_send, NN)
     packet[0] = packed(own_send)
     arrived[OWN] = packed(own)
     arrived[27:32] = jnp.zeros((5, 1, 128), F32)
@@ -178,13 +214,15 @@
     select_deep = jnp.concatenate([select, select], axis=0).astype(BF16)
     unsend = (send_col == lane.astype(F32)).astype(F32)
     spread = (row == lane_atom).astype(F32)
-    centre = dot(own, spread, NN, HIGHEST)
+    centre = pick(own, spread, NN)
 
     slots[...] = jnp.zeros_like(slots)
-    slots[:, 0:ATOMS] = (nbr_ref[0, 0, 0] + 1).astype(F32)
-    named = slots[0:8]
+    for a in range(ATOMS):
+        slots[a : a + 1, 0:SLOTS] = (nbr_ref[0, 0, a] + 1).astype(F32)
+    by_slot = jnp.transpose(slots[...])
+    named = by_slot[0:8]
     for j in range(1, 7):
-        named = named + pltpu.roll(slots[8 * j : 8 * j + 8], ATOMS * j, 1)
+        named = named + pltpu.roll(by_slot[8 * j : 8 * j + 8], ATOMS * j, 1)
     named = named.astype(jnp.int32) - 1
     outer = jnp.maximum(named - ATOMS, 0)
     block = jnp.where(named < 0, -1, jnp.where(named < ATOMS, OWN, over(outer, ATOMS)))
@@ -210,6 +248,8 @@
         bhot[k] = (row[0:32] == block[k : k + 1]).astype(F32)
 
     table_emb[...] = jnp.zeros_like(table_emb)
+    for copy in inputs:
+        copy.wait()
     table_emb[0:89] = emb_ref[...]
     table_emb[128:129, 0:89] = self_ref[...]
     embedding = table_emb[0:128]
@@ -227,17 +267,12 @@
         [rin_high, rin_high, rin_low, jnp.zeros((104, 128), F32)], axis=0
     )
     rin_wide = jnp.transpose(rin_wide)[:, 0:32].astype(BF16)
-    rin_back = []
     rout_wide = []
-    rout_back = []
     for t in range(2):
         high, low = halves(rout_ref[t])
         rout_wide.append(
             jnp.transpose(jnp.concatenate([high, high, low, low], axis=0)).astype(BF16)
         )
-        rout_back.append(jnp.concatenate([high, low], axis=0).astype(BF16))
-        high, low = halves(rin_ref[t])
-        rin_back.append(jnp.concatenate([high, low], axis=0).astype(BF16))
 
     for copy in first:
         copy.wait_recv()
@@ -311,20 +346,23 @@
         harm[:, m, :] = value
 
     basis = jnp.concatenate([basis_ref[k] for k in range(TILES)], axis=1)
-    high, low = halves(basis)
-    basis = jnp.concatenate([high, low, high, jnp.zeros_like(high)], axis=0).astype(BF16)
-    pre = dot(rin_wide, basis, NN)
+
+
+    def radial_in(value):
+        high, low = halves(value)
+        value = jnp.concatenate([high, low, high, jnp.zeros_like(high)], axis=0).astype(BF16)
+        return dot(rin_wide, value, NN)
+
+    pre = radial_in(basis)
     gate = 1.0 / (1.0 + jnp.exp(-pre))
     hidden = pre * gate
     dsilu[...] = gate * (1.0 + pre * (1.0 - gate))
-    hidden_high, hidden_low = halves(hidden)
-
-    def radial_layer(t):
-        rows = slice(HIDDEN * t, HIDDEN * t + HIDDEN)
-        deep = jnp.concatenate(
-            [hidden_high[rows], hidden_low[rows], hidden_high[rows], hidden_low[rows]], axis=0
-        )
-        radial[t] = dot(rout_wide[t], deep.astype(BF16), NN)
+    later[...] = hidden[HIDDEN : 2 * HIDDEN]
+
+    def radial_out(t, value):
+        high, low = halves(value[HIDDEN * t : HIDDEN * t + HIDDEN])
+        deep = jnp.concatenate([high, low, high, low], axis=0).astype(BF16)
+        return dot(rout_wide[t], deep, NN)
 
     def gather_sum(t):
         def chunk(ci, carry):
@@ -335,6 +373,8 @@
                 tile = slice(128 * k, 128 * k + 128)
                 src = source[t, rows[0], tile]
                 terms = [radial[t, rows[q], tile] * src for q in range(3)]
+                term[t, rows[0], tile] = terms[1]
+                term[t, rows[1], tile] = terms[2]
                 ys = harm[k]
                 parts = [terms[0]]
                 parts += [terms[1] * ys[m : m + 1] for m in range(3)]
@@ -359,7 +399,7 @@
         invariants = jnp.concatenate([parts[0], vector, tensor], axis=1)
         return feats + dot_split(invariants, mix_ref[t], NN), parts
 
-    def interaction_back(t, grad, parts, with_source):
+    def interaction_back(t, grad, parts):
         inv_grad = dot_split(grad, mix_ref[t], NT)
         grads = [0.25 * inv_grad[:, 0:128]]
         grads += [0.5 * inv_grad[:, 128:256] * parts[i] for i in range(1, 4)]
@@ -368,54 +408,57 @@
         deep = jnp.concatenate(halves(deep), axis=0).astype(BF16)
         expanded[...] = dot(deep, select_deep, TN).reshape(9, 128, 128)
 
+
+    def source_back():
         def tile_back(k, carry):
             tile = lanes(k)
             ys = harm[k]
-            sums = [jnp.zeros((8, 128), F32)] * 8
             for ci in range(CHANNELS // CHUNK):
                 rows = [slice(128 * q + CHUNK * ci, 128 * q + CHUNK * ci + CHUNK) for q in range(3)]
-                src = source[t, rows[0], tile]
-                rads = [radial[t, rows[q], tile] for q in range(3)]
                 wide = [expanded[i, rows[0], :] for i in range(9)]
                 pulls = [wide[0], wide[1] * ys[0:1], wide[4] * ys[3:4]]
                 for m in range(1, 3):
                     pulls[1] = pulls[1] + wide[1 + m] * ys[m : m + 1]
                 for m in range(4, 8):
                     pulls[2] = pulls[2] + wide[1 + m] * ys[m : m + 1]
-                if with_source:
-                    high, low = halves(
-                        rads[0] * pulls[0] + rads[1] * pulls[1] + rads[2] * pulls[2]
-                    )
-                    source_grad[rows[0], tile] = high.astype(BF16)
-                    source_grad[rows[1], tile] = low.astype(BF16)
-                for q in range(3):
-                    high, low = halves(src * pulls[q])
-                    grad_high[rows[q], tile] = high.astype(BF16)
-                    grad_low[rows[q], tile] = low.astype(BF16)
-                for m in range(8):
-                    value = wide[1 + m] * (rads[1 if m < 3 else 2] * src)
-                    sums[m] = sums[m] + (value[0:8] + value[8:16])
-            tops = [jnp.sum(s, axis=0, keepdims=True) for s in sums]
-            harm_grad[t, k] = jnp.concatenate(tops, axis=0)
+                rads = [radial[1, rows[q], tile] for q in range(3)]
+                high, low = halves(rads[0] * pulls[0] + rads[1] * pulls[1] + rads[2] * pulls[2])
+                source_grad[rows[0], tile] = high.astype(BF16)
+                source_grad[rows[1], tile] = low.astype(BF16)
             return carry
 
         lax.fori_loop(0, TILES, tile_back, 0)
 
-    def radial_back(t):
-        rows = slice(HIDDEN * t, HIDDEN * t + HIDDEN)
-        both = dot(rout_back[t], grad_high[...], NN)
-        grad = both[0:HIDDEN] + both[HIDDEN : 2 * HIDDEN]
-        grad = grad + dot(rout_back[t][0:HIDDEN], grad_low[...], NN)
-        high, low = halves(grad * dsilu[rows])
-        both = dot(rin_back[t], high.astype(BF16), NN)
-        grad = both[0:ORDERS] + both[ORDERS : 2 * ORDERS]
-        grad = grad + dot(rin_back[t][0:ORDERS], low.astype(BF16), NN)
-        for k in range(TILES):
-            r_grad[t, k : k + 1, :] = jnp.sum(
-                grad[:, 128 * k : 128 * k + 128] * dbasis_ref[k], axis=0, keepdims=True
-            )
-
-    radial_layer(0)
+    def edge_back(t):
+        def tile_back(k, carry):
+            tile = lanes(k)
+            ys = harm[k]
+            slopes = [jnp.zeros((8, 128), F32)] * 9
+            sums = [jnp.zeros((8, 128), F32)] * 8
+            for ci in range(CHANNELS // CHUNK):
+                rows = [slice(128 * q + CHUNK * ci, 128 * q + CHUNK * ci + CHUNK) for q in range(3)]
+                src = source[t, rows[0], tile]
+                steep = [slope[t, rows[q], tile] * src for q in range(3)]
+                terms = [term[t, rows[q], tile] for q in range(2)]
+                for m in range(9):
+                    wide = expanded[m, rows[0], :]
+                    q = 0 if m < 1 else 1 if m < 4 else 2
+                    value = wide * steep[q]
+                    slopes[m] = slopes[m] + (value[0:8] + value[8:16])
+                    if m > 0:
+                        value = wide * terms[q - 1]
+                        sums[m - 1] = sums[m - 1] + (value[0:8] + value[8:16])
+            along = slopes[0]
+            for m in range(8):
+                along = along + slopes[1 + m] * ys[m : m + 1]
+            tops = [jnp.sum(s, axis=0, keepdims=True) for s in sums + [along]]
+            tops.append(jnp.zeros((7, 128), F32))
+            edge_grad[t, k] = jnp.concatenate(tops, axis=0)
+            return carry
+
+        lax.fori_loop(0, TILES, tile_back, 0)
+
+    radial[0] = radial_out(0, hidden)
     element = geo[3]
     for k in range(TILES):
         tile = slice(128 * k, 128 * k + 128)
@@ -424,53 +467,58 @@
         source[0, :, tile] = both[0:128] + both[128:256]
     h_one, parts_one = interaction(0, h_zero)
 
-    feat[OWN] = dot_split(h_one, source_ref[1], NN)
-    feat[27] = jnp.zeros((ROWS, 128), F32)
-    second = [
-        remote(1, b, feat.at[OWN], feat.at[b], minus(OFFSETS[b])) for b in OTHERS
-    ]
+    mine[...] = dot_split(h_one, source_ref[1], NN)[0:ATOMS]
+    second = [remote(1, b, mine, feat.at[b], minus(OFFSETS[b])) for b in OTHERS]
     for copy in second:
         copy.start()
-    radial_layer(1)
-    for copy in second:
+    table[...] = jnp.zeros_like(table)
+    table[OWN, 0:ATOMS] = mine[...]
+    later_hidden = jnp.concatenate([later[...], later[...]], axis=0)
+    radial[1] = radial_out(1, later_hidden)
+    tilted = dsilu[...] * radial_in(jnp.concatenate([dbasis_ref[k] for k in range(TILES)], axis=1))
+    slope[0] = radial_out(0, tilted)
+    slope[1] = radial_out(1, tilted)
+    for b, copy in zip(OTHERS[::-1], second[::-1]):
         copy.wait_recv()
-
-    table = jnp.transpose(feat[...].reshape(TABLE, 128))
-    table = jnp.concatenate(halves(table), axis=0).astype(BF16)
-    both = dot(table, onehot[...], NN)
+        table[b, 0:ATOMS] = feat[b]
+
+    turned = jnp.transpose(table[...].reshape(TABLE, 128))
+    turned = jnp.concatenate(halves(turned), axis=0).astype(BF16)
+    both = dot(turned, onehot[...], NN)
     source[1] = both[0:128] + both[128:256]
     h_two, parts_two = interaction(1, h_one)
-    inner = dot_split(h_two, read_hidden_ref[...], NN)
+    inner = dot_split(h_two, read_hidden_ref[...], NT)
     gate = 1.0 / (1.0 + jnp.exp(-inner))
+    inner_grad = gate * (1.0 + inner * (1.0 - gate)) * read_two_ref[...]
+    grad_two = dot_split(inner_grad, read_hidden_ref[...], NN)
+    interaction_back(1, grad_two, parts_two)
+    source_back()
+
+    both = dot(onehot[...], source_grad[...], NT)
+    both = both[:, 0:128] + both[:, 128:256]
+    for b in range(27):
+        feat_grad[b] = both[ROWS * b : ROWS * b + ATOMS]
+    third_copies = [remote(2, b, feat_grad.at[b], feat_back.at[b], OFFSETS[b]) for b in OTHERS]
+    for copy in third_copies:
+        copy.start()
+    edge_back(1)
     learned = jnp.sum(h_one * read_one_ref[...], axis=1, keepdims=True) + jnp.sum(
         inner * gate * read_two_ref[...], axis=1, keepdims=True
     )
     energy = jnp.sum((isolated + learned) * unsend[0:ROWS], axis=0, keepdims=True)
     energy_ref[0, 0] = energy[:, 0:ATOMS]
-    inner_grad = gate * (1.0 + inner * (1.0 - gate)) * read_two_ref[...]
-    grad_two = dot_split(inner_grad, read_hidden_ref[...], NT)
-    interaction_back(1, grad_two, parts_two, True)
-
-    both = dot(onehot[...], source_grad[...], NT)
-    feat_grad[...] = (both[:, 0:128] + both[:, 128:256]).reshape(28, ROWS, 128)
-    third_copies = [
-        remote(2, b, feat_grad.at[b], feat_back.at[b], OFFSETS[b]) for b in OTHERS
-    ]
-    for copy in third_copies:
-        copy.start()
-    radial_back(1)
-    for copy in third_copies:
+    total = feat_grad[OWN]
+    for b, copy in zip(OTHERS[::-1], third_copies[::-1]):
         copy.wait_recv()
-    total = feat_grad[OWN]
-    for b in OTHERS:
         total = total + feat_back[b]
-    grad_one = grad_two + read_one_ref[...] + dot_split(total, source_ref[1], NT)
-
-    interaction_back(0, grad_one, parts_one, False)
-    radial_back(0)
-
-    pulls = [harm_grad[0, :, m, :] + harm_grad[1, :, m, :] for m in range(8)]
-    along = r_grad[0] + r_grad[1]
+    table[OWN, 0:ATOMS] = total
+    grad_one = grad_two + read_one_ref[...] + dot_split(table[OWN], source_ref[1], NT)
+
+    interaction_back(0, grad_one, parts_one)
+    edge_back(0)
+
+    pulls = [edge_grad[0, :, m, :] + edge_grad[1, :, m, :] for m in range(9)]
+    along = pulls[8]
     gx = r3 * pulls[0] + r15 * (ny * pulls[3] + nz * pulls[6] + nx * pulls[7])
     gy = r3 * pulls[1] + r15 * (nx * pulls[3] + nz * pulls[4] - ny * pulls[7])
     gz = r3 * pulls[2] + r15 * (ny * pulls[4] + nx * pulls[6]) + 3.0 * r5 * nz * pulls[5]
@@ -494,7 +542,7 @@
     for copy in fourth:
         copy.start()
     sums = [jnp.sum(p, axis=0, keepdims=True) for p in pulls] + [jnp.zeros((5, 128), F32)]
-    force = dot(jnp.concatenate(sums, axis=0), spread, NT, HIGHEST)
+    force = pick(jnp.concatenate(sums, axis=0), spread, NT)
     own_row = rows[OWN : OWN + 1]
     force = force - jnp.concatenate([unrolled(own_row, c) for c in range(3)] + [sums[3]], axis=0)
     for copy in fourth:
@@ -503,8 +551,9 @@
     for b in OTHERS[1:]:
         back = back + returned[b]
     back = jnp.concatenate([unrolled(back, c) for c in range(3)] + [sums[3]], axis=0)
-    force = force - dot(back, unsend, NN, HIGHEST)
-    force_ref[0, 0, 0] = force[0:3, 0:ATOMS]
+    force = force - pick(back, unsend, NN)
+    for c in range(3):
+        force_ref[0, 0, c] = force[c : c + 1, 0:ATOMS]
     for copy in first + second + third_copies + fourth:
         copy.wait_send()
 
@@ -525,25 +574,33 @@
     read_two,
 ):
     vmem = pl.BlockSpec(memory_space=pltpu.VMEM)
+    hbm = pl.BlockSpec(memory_space=pltpu.HBM)
     energy, forces = pl.pallas_call(
         kernel,
         out_shape=(
             jax.ShapeDtypeStruct((1, 1, 1, ATOMS), F32),
-            jax.ShapeDtypeStruct((1, 1, 1, 3, ATOMS), F32),
+            jax.ShapeDtypeStruct((1, 1, 3, 1, ATOMS), F32),
         ),
-        in_specs=[vmem] * 13,
+        in_specs=[vmem] * 4 + [hbm, vmem] + [hbm] * 4 + [vmem] * 3,
         out_specs=(vmem, vmem),
         scratch_shapes=[
+            pltpu.VMEM(embedding.shape, F32),
+            pltpu.VMEM(source_weight.shape, F32),
+            pltpu.VMEM(radial_in.shape, F32),
+            pltpu.VMEM(radial_out.shape, F32),
+            pltpu.VMEM(mix_weight.shape, F32),
             pltpu.VMEM((16, 128), F32),
-            pltpu.VMEM((SLOTS, 128), F32),
+            pltpu.VMEM((128, 128), F32),
             pltpu.VMEM((136, 128), F32),
             pltpu.VMEM((1, 1, 128), F32),
             pltpu.VMEM((32, 1, 128), F32),
             pltpu.VMEM((27, 1, 128), F32),
             pltpu.VMEM((27, 1, 128), F32),
+            pltpu.VMEM((ATOMS, 128), F32),
+            pltpu.VMEM((27, ATOMS, 128), F32),
             pltpu.VMEM((28, ROWS, 128), F32),
-            pltpu.VMEM((28, ROWS, 128), F32),
-            pltpu.VMEM((27, ROWS, 128), F32),
+            pltpu.VMEM((27, ATOMS, 128), F32),
+            pltpu.VMEM((27, ATOMS, 128), F32),
             pltpu.VMEM((TABLE, EDGES), BF16),
             pltpu.VMEM((128, EDGES), BF16),
             pltpu.VMEM((TILES, 32, 128), F32),
@@ -551,28 +608,29 @@
             pltpu.VMEM((TILES, ORDERS, 128), F32),
             pltpu.VMEM((TILES, ORDERS, 128), F32),
             pltpu.VMEM((TILES, 8, 128), F32),
-            pltpu.VMEM((2, TILES, 8, 128), F32),
-            pltpu.VMEM((2, TILES, 128), F32),
+            pltpu.VMEM((2, TILES, 16, 128), F32),
             pltpu.VMEM((2, 384, EDGES), F32),
+            pltpu.VMEM((2, 384, EDGES), F32),
+            pltpu.VMEM((2, 256, EDGES), F32),
             pltpu.VMEM((128, EDGES), F32),
+            pltpu.VMEM((HIDDEN, EDGES), F32),
             pltpu.VMEM((2, 128, EDGES), F32),
             pltpu.VMEM((256, EDGES), BF16),
             pltpu.VMEM((9, 128, 128), F32),
             pltpu.VMEM((9, 128, 128), F32),
-            pltpu.VMEM((384, EDGES), BF16),
-            pltpu.VMEM((384, EDGES), BF16),
             pltpu.SemaphoreType.DMA((4, 27)),
             pltpu.SemaphoreType.DMA((4, 27)),
+            pltpu.SemaphoreType.DMA((5,)),
         ],
         compiler_params=pltpu.CompilerParams(
-            collective_id=0, has_side_effects=True, vmem_limit_bytes=48 * 1024 * 1024
+            collective_id=0, has_side_effects=True, vmem_limit_bytes=55168 * 1024
         ),
         name="energy_and_forces",
     )(
-        positions,
+        positions.transpose(0, 1, 3, 2, 4),
         species,
         send_rows,
-        neighbours,
+        neighbours.transpose(0, 1, 4, 2, 3),
         embedding,
         self_energy[None],
         source_weight,
@@ -580,10 +638,10 @@
         radial_out,
         mix_weight,
         read_one[None],
-        read_hidden,
+        read_hidden.T,
         read_two[None],
     )
-    return energy, forces
+    return energy, forces.transpose(0, 1, 3, 2, 4)
 
 
 def solution(mesh):

time: 76.3 us -> 69.7 us (0.913)
  Pallas kernels: 69.9 us -> 62.9 us
    pallas_call x1, Pallas kernels: 69.9 us -> 62.9 us  [per_device(): pl.pallas_call(kernel, out_shape=(jax.ShapeDtypeStruct((1, 1, 1, ATOMS),...]
    unnamed x28 -> x20, local copies, waits for them, and re-layouts: 4.8 us -> 5.77 us
where the time goes in v1:
time: 69.7 us; the launch traced here: 69.4 us
  Pallas kernels  62.9 us (90%)
  local copies, waits for them, and re-layouts  5.77 us (8%)
    pallas_call x1, Pallas kernels, per_device(): pl.pallas_call(kernel, out_shape=(jax.ShapeDtypeStruct((1, 1, 1, ATOMS),...  62.9 us
    unnamed x20, local copies, waits for them, and re-layouts  5.77 us

profile of v1, /device:TPU:1, one launch (start us, length us, event | category | flops | bytes accessed | tf_op | source)
XLA Modules:
  0.0 69.4 jit_solution(3606167827866204795)
XLA Ops:
  0.6 0.0 copy-start
  0.6 0.0 copy-start.3
  0.7 0.0 copy-start.4
  0.7 0.7 copy-done
  1.3 0.0 copy-done.3
  1.3 0.0 copy-done.4
  1.3 0.0 copy-start.1
  1.3 0.7 %copy-done.1 = f32[2,8,64]{2,1,0:T(8,128)S(1)} copy-done((f32[2,8,64]{2,1,0:T(8,128)S(1)}, f32[2,8,64]{2,1,0:T(8,128)}, u32[]{:S(2)}) %copy-start.1) | copy-done | bytes 4120
  2.0 0.0 copy-start.2
  2.0 0.7 %copy-done.2 = f32[128,16]{0,1:T(8,128)S(1)} copy-done((f32[128,16]{0,1:T(8,128)S(1)}, f32[128,16]{0,1:T(8,128)}, u32[]{:S(2)}) %copy-start.2) | copy-done | bytes 8216
  2.7 0.0 copy-start.5
  2.7 0.7 copy-done.5
  3.4 0.0 copy-start.6
  3.4 0.7 copy-done.6
  4.0 0.0 copy-start.7
  4.1 0.7 copy-done.7
  4.7 0.0 copy-start.8
  4.7 0.7 copy-done.8
  5.4 62.9 %energy_and_forces.1 = (f32[1,1,1,18]{3,2,1,0:T(1,128)S(1)}, f32[1,1,3,1,18]{4,3,2,1,0:T(1,128)S(1)}) custom-call(f32[1,1,3,1,18]{4,3,2,1,0:T(1,128)S(1)} %bitcast.9, s32[1,1,1,18]{3,2,1,0:T(1,128)S(1)} %copy-done.4, s32[1,1,1,18]{3,2,1,0:T(1,128)S(1)} %copy-done.5, s32[1,1,18,1,56]{4,3,2,1,0:T(1,128)S(1)} %bitcast.7, f32[89,128]{1,0:T(8,128)} %emb_hbm.1, ...), custom_call_target="tpu_custom_call" | custom-call | tf_op jit(solution)/shard_map/energy_and_forces/pallas_call | solution.py:578
  68.3 0.5 copy.17
  68.8 0.6 copy.18
Async XLA Ops:
  0.6 0.7 %copy-start = (s32[1,1,1,56,18]{3,2,4,1,0:T(1,128)S(1)}, s32[1,1,1,56,18]{3,2,4,1,0:T(1,128)}, u32[]{:S(2)}) copy-start(s32[1,1,1,56,18]{3,2,4,1,0:T(1,128)} %param.16) | copy-start | bytes 12100
  0.6 0.7 copy-start.3
  0.7 0.7 copy-start.4
  1.3 0.7 %copy-start.1 = (f32[2,8,64]{2,1,0:T(8,128)S(1)}, f32[2,8,64]{2,1,0:T(8,128)}, u32[]{:S(2)}) copy-start(f32[2,8,64]{2,1,0:T(8,128)} %rin_hbm.1) | copy-start | bytes 12292
  2.0 0.7 %copy-start.2 = (f32[128,16]{0,1:T(8,128)S(1)}, f32[128,16]{0,1:T(8,128)}, u32[]{:S(2)}) copy-start(f32[128,16]{0,1:T(8,128)} %param.24) | copy-start | bytes 24580
  2.7 0.7 copy-start.5
  3.4 0.7 copy-start.6
  4.0 0.7 copy-start.7
  4.7 0.7 copy-start.8

commit v2 on v1

--- a/solution.py
+++ b/solution.py
@@ -68,6 +68,17 @@
     )
 
 
+def parted(value, axis):
+    return jnp.concatenate(halves(value), axis=axis).astype(BF16)
+
+
+def apply(left, right, dims):
+    both = dot(parted(left, 0), right, dims)
+    both = both[0:ROWS] + both[ROWS : 2 * ROWS]
+    half = both.shape[1] // 2
+    return both[:, 0:half] + both[:, half:]
+
+
 def iota(shape, dim):
     return lax.broadcasted_iota(jnp.int32, shape, dim)
 
@@ -96,26 +107,34 @@
 
 
 def kernel(
+    pos_hbm,
+    species_hbm,
+    send_hbm,
+    nbr_hbm,
+    emb_hbm,
+    self_hbm,
+    source_hbm,
+    rin_hbm,
+    rout_hbm,
+    mix_hbm,
+    read_one_hbm,
+    read_hidden_hbm,
+    read_two_hbm,
+    energy_ref,
+    force_ref,
     pos_ref,
     species_ref,
     send_ref,
     nbr_ref,
-    emb_hbm,
+    emb_ref,
     self_ref,
-    source_hbm,
-    rin_hbm,
-    rout_hbm,
-    mix_hbm,
-    read_one_ref,
-    read_hidden_ref,
-    read_two_ref,
-    energy_ref,
-    force_ref,
-    emb_ref,
     source_ref,
     rin_ref,
     rout_ref,
     mix_ref,
+    read_one_ref,
+    read_hidden_ref,
+    read_two_ref,
     stage,
     slots,
     table_emb,
@@ -130,6 +149,7 @@
     feat_back,
     onehot,
     ghot,
+    gdeep,
     bhot,
     geo,
     basis_ref,
@@ -162,18 +182,28 @@
         pltpu.make_async_copy(src, dst, loaded.at[i])
         for i, (src, dst) in enumerate(
             (
+                (pos_hbm, pos_ref),
+                (species_hbm, species_ref),
+                (send_hbm, send_ref),
+                (nbr_hbm, nbr_ref),
                 (emb_hbm, emb_ref),
+                (self_hbm, self_ref),
                 (source_hbm, source_ref),
                 (rin_hbm, rin_ref),
                 (rout_hbm, rout_ref),
                 (mix_hbm, mix_ref),
+                (read_one_hbm, read_one_ref),
+                (read_hidden_hbm, read_hidden_ref),
+                (read_two_hbm, read_two_ref),
             )
         )
     ]
+    for copy in inputs[0:3]:
+        copy.start()
     barrier = pltpu.get_barrier_semaphore()
     for b in OTHERS:
         pl.semaphore_signal(barrier, inc=1, device_id=device(OFFSETS[b]), device_id_type=MESH)
-    for copy in inputs:
+    for copy in inputs[3:]:
         copy.start()
 
     def remote(phase, index, src, dst, offset):
@@ -187,6 +217,8 @@
         )
 
     stage[...] = jnp.zeros_like(stage)
+    for copy in inputs[0:3]:
+        copy.wait()
     for c in range(3):
         stage[c : c + 1, 0:ATOMS] = pos_ref[0, 0, c]
     stage[3:4, 0:ATOMS] = species_ref[0, 0].astype(F32)
@@ -217,6 +249,7 @@
     centre = pick(own, spread, NN)
 
     slots[...] = jnp.zeros_like(slots)
+    inputs[3].wait()
     for a in range(ATOMS):
         slots[a : a + 1, 0:SLOTS] = (nbr_ref[0, 0, a] + 1).astype(F32)
     by_slot = jnp.transpose(slots[...])
@@ -248,7 +281,7 @@
         bhot[k] = (row[0:32] == block[k : k + 1]).astype(F32)
 
     table_emb[...] = jnp.zeros_like(table_emb)
-    for copy in inputs:
+    for copy in inputs[4:]:
         copy.wait()
     table_emb[0:89] = emb_ref[...]
     table_emb[128:129, 0:89] = self_ref[...]
@@ -273,6 +306,18 @@
         rout_wide.append(
             jnp.transpose(jnp.concatenate([high, high, low, low], axis=0)).astype(BF16)
         )
+
+    read_hidden = read_hidden_ref[...]
+    chain = dot_split(mix_ref[0], source_ref[1], NN)
+    chain_wide = parted(chain, 1)
+    chain_deep = parted(chain, 0)
+    read_in = parted(dot_split(mix_ref[1], read_hidden, NT), 1)
+    read_out = parted(dot_split(read_hidden, mix_ref[1], NT), 1)
+    zero_source = dot_split(h_zero, source_ref[1], NN)
+    for k in range(TILES):
+        tile = slice(128 * k, 128 * k + 128)
+        repeated = jnp.where(row < 96, row - 32 * over(row, 32), -3)
+        gdeep[:, tile] = (repeated == member[k : k + 1]).astype(F32).astype(BF16)
 
     for copy in first:
         copy.wait_recv()
@@ -290,11 +335,10 @@
     )
     nearby = arrived[...].reshape(32, 128) + shift
     nearby = jnp.concatenate([unrolled(nearby, c) for c in range(4)], axis=0)
-    high, low = halves(nearby)
+    high, low = halves(jnp.where(lane < 32, nearby, 0.0))
     middle, low = halves(low)
-    nearby = jnp.concatenate([high, middle, low], axis=0).astype(BF16)
-    by_block = dot(nearby, ghot[...], NN)
-    by_block = by_block[0:128] + by_block[128:256] + by_block[256:384]
+    nearby = high + pltpu.roll(middle, 32, 1) + pltpu.roll(low, 64, 1)
+    by_block = dot(nearby.astype(BF16), gdeep[...], NN)
     for k in range(TILES):
         tile = slice(128 * k, 128 * k + 128)
         for c in range(4):
@@ -347,7 +391,6 @@
 
     basis = jnp.concatenate([basis_ref[k] for k in range(TILES)], axis=1)
 
-
     def radial_in(value):
         high, low = halves(value)
         value = jnp.concatenate([high, low, high, jnp.zeros_like(high)], axis=0).astype(BF16)
@@ -386,7 +429,7 @@
 
         lax.fori_loop(0, CHANNELS // CHUNK, chunk, 0)
 
-    def interaction(t, feats):
+    def interaction(t):
         gather_sum(t)
         wide = acc[...].reshape(9 * 128, 128)
         wide = jnp.concatenate(halves(wide), axis=1).astype(BF16)
@@ -396,18 +439,15 @@
         tensor = parts[4] * parts[4]
         for i in range(5, 9):
             tensor = tensor + parts[i] * parts[i]
-        invariants = jnp.concatenate([parts[0], vector, tensor], axis=1)
-        return feats + dot_split(invariants, mix_ref[t], NN), parts
-
-    def interaction_back(t, grad, parts):
-        inv_grad = dot_split(grad, mix_ref[t], NT)
+        return jnp.concatenate([parts[0], vector, tensor], axis=1), parts
+
+    def interaction_back(inv_grad, parts):
         grads = [0.25 * inv_grad[:, 0:128]]
         grads += [0.5 * inv_grad[:, 128:256] * parts[i] for i in range(1, 4)]
         grads += [0.5 * inv_grad[:, 256:384] * parts[i] for i in range(4, 9)]
         deep = jnp.concatenate(grads, axis=1)
         deep = jnp.concatenate(halves(deep), axis=0).astype(BF16)
         expanded[...] = dot(deep, select_deep, TN).reshape(9, 128, 128)
-
 
     def source_back():
         def tile_back(k, carry):
@@ -438,7 +478,9 @@
             for ci in range(CHANNELS // CHUNK):
                 rows = [slice(128 * q + CHUNK * ci, 128 * q + CHUNK * ci + CHUNK) for q in range(3)]
                 src = source[t, rows[0], tile]
-                steep = [slope[t, rows[q], tile] * src for q in range(3)]
+                steep = [slope[t, rows[q], tile] for q in range(3)]
+                if t == 1:
+                    steep = [value * src for value in steep]
                 terms = [term[t, rows[q], tile] for q in range(2)]
                 for m in range(9):
                     wide = expanded[m, rows[0], :]
@@ -465,18 +507,22 @@
         hot = (row.astype(F32) == element[k : k + 1]).astype(F32).astype(BF16)
         both = dot(emb_source, hot, NN)
         source[0, :, tile] = both[0:128] + both[128:256]
-    h_one, parts_one = interaction(0, h_zero)
-
-    mine[...] = dot_split(h_one, source_ref[1], NN)[0:ATOMS]
+    invariants, parts_one = interaction(0)
+
+    mine[...] = (zero_source + apply(invariants, chain_wide, NN))[0:ATOMS]
     second = [remote(1, b, mine, feat.at[b], minus(OFFSETS[b])) for b in OTHERS]
     for copy in second:
         copy.start()
     table[...] = jnp.zeros_like(table)
     table[OWN, 0:ATOMS] = mine[...]
+    h_one = h_zero + dot_split(invariants, mix_ref[0], NN)
+    read_one = dot_split(h_one, read_hidden, NT)
     later_hidden = jnp.concatenate([later[...], later[...]], axis=0)
     radial[1] = radial_out(1, later_hidden)
     tilted = dsilu[...] * radial_in(jnp.concatenate([dbasis_ref[k] for k in range(TILES)], axis=1))
-    slope[0] = radial_out(0, tilted)
+    steep = radial_out(0, tilted)
+    for q in range(3):
+        slope[0, 128 * q : 128 * q + 128] = steep[128 * q : 128 * q + 128] * source[0]
     slope[1] = radial_out(1, tilted)
     for b, copy in zip(OTHERS[::-1], second[::-1]):
         copy.wait_recv()
@@ -486,12 +532,11 @@
     turned = jnp.concatenate(halves(turned), axis=0).astype(BF16)
     both = dot(turned, onehot[...], NN)
     source[1] = both[0:128] + both[128:256]
-    h_two, parts_two = interaction(1, h_one)
-    inner = dot_split(h_two, read_hidden_ref[...], NT)
+    invariants, parts_two = interaction(1)
+    inner = read_one + apply(invariants, read_in, NN)
     gate = 1.0 / (1.0 + jnp.exp(-inner))
     inner_grad = gate * (1.0 + inner * (1.0 - gate)) * read_two_ref[...]
-    grad_two = dot_split(inner_grad, read_hidden_ref[...], NN)
-    interaction_back(1, grad_two, parts_two)
+    interaction_back(apply(inner_grad, read_out, NN), parts_two)
     source_back()
 
     both = dot(onehot[...], source_grad[...], NT)
@@ -501,20 +546,22 @@
     third_copies = [remote(2, b, feat_grad.at[b], feat_back.at[b], OFFSETS[b]) for b in OTHERS]
     for copy in third_copies:
         copy.start()
+    grad_two = dot_split(inner_grad, read_hidden, NN) + read_one_ref[...]
+    grad_two = dot_split(grad_two, mix_ref[0], NT)
     edge_back(1)
     learned = jnp.sum(h_one * read_one_ref[...], axis=1, keepdims=True) + jnp.sum(
         inner * gate * read_two_ref[...], axis=1, keepdims=True
     )
     energy = jnp.sum((isolated + learned) * unsend[0:ROWS], axis=0, keepdims=True)
-    energy_ref[0, 0] = energy[:, 0:ATOMS]
+    energy_ref[0, 0] = -energy[:, 0:ATOMS]
     total = feat_grad[OWN]
     for b, copy in zip(OTHERS[::-1], third_copies[::-1]):
         copy.wait_recv()
         total = total + feat_back[b]
     table[OWN, 0:ATOMS] = total
-    grad_one = grad_two + read_one_ref[...] + dot_split(table[OWN], source_ref[1], NT)
-
-    interaction_back(0, grad_one, parts_one)
+    grad_one = grad_two + apply(table[OWN], chain_deep, NT)
+
+    interaction_back(grad_one, parts_one)
     edge_back(0)
 
     pulls = [edge_grad[0, :, m, :] + edge_grad[1, :, m, :] for m in range(9)]
@@ -544,14 +591,14 @@
     sums = [jnp.sum(p, axis=0, keepdims=True) for p in pulls] + [jnp.zeros((5, 128), F32)]
     force = pick(jnp.concatenate(sums, axis=0), spread, NT)
     own_row = rows[OWN : OWN + 1]
-    force = force - jnp.concatenate([unrolled(own_row, c) for c in range(3)] + [sums[3]], axis=0)
+    force = jnp.concatenate([unrolled(own_row, c) for c in range(3)] + [sums[3]], axis=0) - force
     for copy in fourth:
         copy.wait_recv()
     back = returned[OTHERS[0]]
     for b in OTHERS[1:]:
         back = back + returned[b]
     back = jnp.concatenate([unrolled(back, c) for c in range(3)] + [sums[3]], axis=0)
-    force = force - pick(back, unsend, NN)
+    force = force + pick(back, unsend, NN)
     for c in range(3):
         force_ref[0, 0, c] = force[c : c + 1, 0:ATOMS]
     for copy in first + second + third_copies + fourth:
@@ -574,21 +621,28 @@
     read_two,
 ):
     vmem = pl.BlockSpec(memory_space=pltpu.VMEM)
-    hbm = pl.BlockSpec(memory_space=pltpu.HBM)
     energy, forces = pl.pallas_call(
         kernel,
         out_shape=(
             jax.ShapeDtypeStruct((1, 1, 1, ATOMS), F32),
             jax.ShapeDtypeStruct((1, 1, 3, 1, ATOMS), F32),
         ),
-        in_specs=[vmem] * 4 + [hbm, vmem] + [hbm] * 4 + [vmem] * 3,
+        in_specs=[pl.BlockSpec(memory_space=pltpu.HBM)] * 13,
         out_specs=(vmem, vmem),
         scratch_shapes=[
+            pltpu.VMEM((1, 1, 3, 1, ATOMS), F32),
+            pltpu.VMEM((1, 1, 1, ATOMS), jnp.int32),
+            pltpu.VMEM((1, 1, 1, ATOMS), jnp.int32),
+            pltpu.VMEM((1, 1, ATOMS, 1, SLOTS), jnp.int32),
             pltpu.VMEM(embedding.shape, F32),
+            pltpu.VMEM((1, 89), F32),
             pltpu.VMEM(source_weight.shape, F32),
             pltpu.VMEM(radial_in.shape, F32),
             pltpu.VMEM(radial_out.shape, F32),
             pltpu.VMEM(mix_weight.shape, F32),
+            pltpu.VMEM((1, 128), F32),
+            pltpu.VMEM((16, 128), F32),
+            pltpu.VMEM((1, 16), F32),
             pltpu.VMEM((16, 128), F32),
             pltpu.VMEM((128, 128), F32),
             pltpu.VMEM((136, 128), F32),
@@ -602,6 +656,7 @@
             pltpu.VMEM((27, ATOMS, 128), F32),
             pltpu.VMEM((27, ATOMS, 128), F32),
             pltpu.VMEM((TABLE, EDGES), BF16),
+            pltpu.VMEM((128, EDGES), BF16),
             pltpu.VMEM((128, EDGES), BF16),
             pltpu.VMEM((TILES, 32, 128), F32),
             pltpu.VMEM((4, 8, 128), F32),
@@ -620,10 +675,10 @@
             pltpu.VMEM((9, 128, 128), F32),
             pltpu.SemaphoreType.DMA((4, 27)),
             pltpu.SemaphoreType.DMA((4, 27)),
-            pltpu.SemaphoreType.DMA((5,)),
+            pltpu.SemaphoreType.DMA((13,)),
         ],
         compiler_params=pltpu.CompilerParams(
-            collective_id=0, has_side_effects=True, vmem_limit_bytes=55168 * 1024
+            collective_id=0, has_side_effects=True, vmem_limit_bytes=60 * 1024 * 1024
         ),
         name="energy_and_forces",
     )(
@@ -641,7 +696,7 @@
         read_hidden.T,
         read_two[None],
     )
-    return energy, forces.transpose(0, 1, 3, 2, 4)
+    return -energy, -forces.transpose(0, 1, 3, 2, 4)
 
 
 def solution(mesh):

time: 69.7 us -> 65.2 us (0.935)
  local copies, waits for them, and re-layouts: 5.77 us -> 0.62 us
  other arithmetic: 0 us -> 1.08 us
    unnamed x20 -> x4, local copies, waits for them, and re-layouts: 5.77 us -> 0.62 us
    neg x0 -> x2, other arithmetic: none -> 1.08 us  [per_device(): return (-energy, -forces.transpose(0, 1, 3, 2, 4))]
where the time goes in v2:
time: 65.2 us; the launch traced here: 65 us
  Pallas kernels  62.7 us (96%)
  other arithmetic  1.08 us (2%)
  between operations  0.66 us (1%)
    pallas_call x1, Pallas kernels, per_device(): pl.pallas_call(kernel, out_shape=(jax.ShapeDtypeStruct((1, 1, 1, ATOMS),...  62.7 us

profile of v2, /device:TPU:1, one launch (start us, length us, event | category | flops | bytes accessed | tf_op | source)
XLA Modules:
  0.0 65.0 jit_solution(17821029622592268011)
XLA Ops:
  0.6 62.7 %energy_and_forces.1 = (f32[1,1,1,18]{3,2,1,0:T(1,128)}, f32[1,1,3,1,18]{4,3,2,1,0:T(1,128)}) custom-call(f32[1,1,3,1,18]{4,3,2,1,0:T(1,128)} %bitcast.10, s32[1,1,1,18]{3,2,1,0:T(1,128)} %species_hbm.1, s32[1,1,1,18]{3,2,1,0:T(1,128)} %send_hbm.1, s32[1,1,18,1,56]{4,3,2,1,0:T(1,128)} %bitcast.8, f32[89,128]{1,0:T(8,128)} %emb_hbm.1, f32[1,89]{1,0:T(1,128)} %bitcast.11, ...), custom_call_target="tpu_custom_call" | custom-call | tf_op jit(solution)/shard_map/energy_and_forces/pallas_call | solution.py:624
  63.3 0.0 copy-start.1
  63.3 0.0 copy-start
  63.3 0.6 copy-done.1
  63.9 0.5 neg.17
  64.5 0.0 copy-done
  64.5 0.6 negate_bitcast_fusion
Async XLA Ops:
  63.3 0.6 copy-start.1
  63.3 1.1 %copy-start = (f32[1,1,3,1,18]{4,3,2,1,0:T(1,128)S(1)}, f32[1,1,3,1,18]{4,3,2,1,0:T(1,128)}, u32[]{:S(2)}) copy-start(f32[1,1,3,1,18]{4,3,2,1,0:T(1,128)} %get-tuple-element.5) | copy-start | bytes 652

commit v3 on v2

--- a/solution.py
+++ b/solution.py
@@ -20,7 +20,7 @@
 HIDDEN = 64
 ORDERS = 8
 ROWS = 24
-TABLE = 28 * ROWS
+GROUP = 256
 EDGES = 1024
 TILES = 8
 CHUNK = 16
@@ -32,6 +32,7 @@
         key=lambda b: -sum(abs(o) * w for o, w in zip(OFFSETS[b], (2, 1, 4))),
     )
 )
+PLACES = (0, 1, 2, 3, 5, 6, 7, 8)
 NN = ((1,), (0,))
 NT = ((1,), (1,))
 TN = ((0,), (0,))
@@ -206,6 +207,8 @@
     for copy in inputs[3:]:
         copy.start()
 
+    across = jnp.where(lax.rem(me[2], 4) < 2, -1, 1)
+
     def remote(phase, index, src, dst, offset):
         return pltpu.make_async_remote_copy(
             src_ref=src,
@@ -262,21 +265,23 @@
     member = jnp.where(named < ATOMS, named, outer - ATOMS * over(outer, ATOMS))
     usable = (named >= 0).astype(F32)
 
-    table_row = iota((TABLE, 128), 0)
-    table_block = over(table_row, ROWS)
-    table_member = table_row - ROWS * table_block
-    label = jnp.where(
-        (table_member < ATOMS) & (table_block < 27),
-        ATOMS + ATOMS * table_block + table_member,
-        -2,
-    )
-    label = jnp.concatenate(
-        [label[0 : OWN * ROWS], send_col[0:ROWS].astype(jnp.int32), label[(OWN + 1) * ROWS :]],
-        axis=0,
-    )
+    table_row = iota((GROUP, 128), 0)
+    table_place = over(table_row, ROWS)
+    table_member = table_row - ROWS * table_place
+    held = (table_member < ATOMS) & (table_place < 9)
+    for q in range(3):
+        label = ATOMS + ATOMS * (3 * table_place + q) + table_member
+        label = jnp.where(held, label, -2)
+        if q == 1:
+            label = jnp.concatenate(
+                [label[0 : 4 * ROWS], send_col[0:ROWS].astype(jnp.int32), label[5 * ROWS :]],
+                axis=0,
+            )
+        for k in range(TILES):
+            tile = slice(128 * k, 128 * k + 128)
+            onehot[q, :, tile] = (label == named[k : k + 1]).astype(F32).astype(BF16)
     for k in range(TILES):
         tile = slice(128 * k, 128 * k + 128)
-        onehot[:, tile] = (label == named[k : k + 1]).astype(F32).astype(BF16)
         ghot[:, tile] = (row == member[k : k + 1]).astype(F32).astype(BF16)
         bhot[k] = (row[0:32] == block[k : k + 1]).astype(F32)
 
@@ -510,11 +515,20 @@
     invariants, parts_one = interaction(0)
 
     mine[...] = (zero_source + apply(invariants, chain_wide, NN))[0:ATOMS]
-    second = [remote(1, b, mine, feat.at[b], minus(OFFSETS[b])) for b in OTHERS]
-    for copy in second:
-        copy.start()
+
+    def second(place, level):
+        offset = (place // 3 - 1, place % 3 - 1, level)
+        slot = 9 * (1 - level) + 8 - place
+        return remote(1, slot, mine, feat.at[1 - level, 8 - place], offset)
+
+    for place in range(9):
+        second(place, across).start()
+    for place in range(9):
+        second(place, -across).start()
+    for place in PLACES:
+        second(place, 0).start()
     table[...] = jnp.zeros_like(table)
-    table[OWN, 0:ATOMS] = mine[...]
+    table[1, 4 * ROWS : 4 * ROWS + ATOMS] = mine[...]
     h_one = h_zero + dot_split(invariants, mix_ref[0], NN)
     read_one = dot_split(h_one, read_hidden, NT)
     later_hidden = jnp.concatenate([later[...], later[...]], axis=0)
@@ -524,14 +538,19 @@
     for q in range(3):
         slope[0, 128 * q : 128 * q + 128] = steep[128 * q : 128 * q + 128] * source[0]
     slope[1] = radial_out(1, tilted)
-    for b, copy in zip(OTHERS[::-1], second[::-1]):
-        copy.wait_recv()
-        table[b, 0:ATOMS] = feat[b]
-
-    turned = jnp.transpose(table[...].reshape(TABLE, 128))
-    turned = jnp.concatenate(halves(turned), axis=0).astype(BF16)
-    both = dot(turned, onehot[...], NN)
-    source[1] = both[0:128] + both[128:256]
+
+    def gather(level, places):
+        for place in places:
+            second(8 - place, -level).wait_recv()
+            table[1 + level, ROWS * place : ROWS * place + ATOMS] = feat[1 + level, place]
+        turned = parted(jnp.transpose(table[1 + level]), 0)
+        both = dot(turned, onehot[1 + level], NN)
+        return both[0:128] + both[128:256]
+
+    source[1] = gather(0, PLACES)
+    source[1] = source[1] + gather(-across, range(9))
+    source[1] = source[1] + gather(across, range(9))
+
     invariants, parts_two = interaction(1)
     inner = read_one + apply(invariants, read_in, NN)
     gate = 1.0 / (1.0 + jnp.exp(-inner))
@@ -539,13 +558,22 @@
     interaction_back(apply(inner_grad, read_out, NN), parts_two)
     source_back()
 
-    both = dot(onehot[...], source_grad[...], NT)
-    both = both[:, 0:128] + both[:, 128:256]
-    for b in range(27):
-        feat_grad[b] = both[ROWS * b : ROWS * b + ATOMS]
-    third_copies = [remote(2, b, feat_grad.at[b], feat_back.at[b], OFFSETS[b]) for b in OTHERS]
-    for copy in third_copies:
-        copy.start()
+    def third(place, level):
+        offset = (place // 3 - 1, place % 3 - 1, level)
+        slot = 9 * (1 + level) + place
+        return remote(2, slot, feat_grad.at[1 + level, place], feat_back.at[1 + level, place], offset)
+
+    def scatter(level, places):
+        both = dot(onehot[1 + level], source_grad[...], NT)
+        both = both[:, 0:128] + both[:, 128:256]
+        for place in range(9):
+            feat_grad[1 + level, place] = both[ROWS * place : ROWS * place + ATOMS]
+        for place in places:
+            third(place, level).start()
+
+    scatter(across, range(9))
+    scatter(-across, range(9))
+    scatter(0, PLACES)
     grad_two = dot_split(inner_grad, read_hidden, NN) + read_one_ref[...]
     grad_two = dot_split(grad_two, mix_ref[0], NT)
     edge_back(1)
@@ -554,12 +582,14 @@
     )
     energy = jnp.sum((isolated + learned) * unsend[0:ROWS], axis=0, keepdims=True)
     energy_ref[0, 0] = -energy[:, 0:ATOMS]
-    total = feat_grad[OWN]
-    for b, copy in zip(OTHERS[::-1], third_copies[::-1]):
-        copy.wait_recv()
-        total = total + feat_back[b]
-    table[OWN, 0:ATOMS] = total
-    grad_one = grad_two + apply(table[OWN], chain_deep, NT)
+    total = feat_grad[1, 4]
+    for level, places in ((0, PLACES), (across, range(9)), (-across, range(9))):
+        for place in places:
+            third(place, level).wait_recv()
+            total = total + feat_back[1 + level, place]
+    own_rows = slice(4 * ROWS, 4 * ROWS + ROWS)
+    table[1, 4 * ROWS : 4 * ROWS + ATOMS] = total
+    grad_one = grad_two + apply(table[1, own_rows], chain_deep, NT)
 
     interaction_back(grad_one, parts_one)
     edge_back(0)
@@ -601,8 +631,12 @@
     force = force + pick(back, unsend, NN)
     for c in range(3):
         force_ref[0, 0, c] = force[c : c + 1, 0:ATOMS]
-    for copy in first + second + third_copies + fourth:
+    for copy in first + fourth:
         copy.wait_send()
+    for level in range(-1, 2):
+        for place in PLACES if level == 0 else range(9):
+            second(place, level).wait_send()
+            third(place, level).wait_send()
 
 
 def per_device(
@@ -651,11 +685,11 @@
             pltpu.VMEM((27, 1, 128), F32),
             pltpu.VMEM((27, 1, 128), F32),
             pltpu.VMEM((ATOMS, 128), F32),
-            pltpu.VMEM((27, ATOMS, 128), F32),
-            pltpu.VMEM((28, ROWS, 128), F32),
-            pltpu.VMEM((27, ATOMS, 128), F32),
-            pltpu.VMEM((27, ATOMS, 128), F32),
-            pltpu.VMEM((TABLE, EDGES), BF16),
+            pltpu.VMEM((3, 9, ATOMS, 128), F32),
+            pltpu.VMEM((3, GROUP, 128), F32),
+            pltpu.VMEM((3, 9, ATOMS, 128), F32),
+            pltpu.VMEM((3, 9, ATOMS, 128), F32),
+            pltpu.VMEM((3, GROUP, EDGES), BF16),
             pltpu.VMEM((128, EDGES), BF16),
             pltpu.VMEM((128, EDGES), BF16),
             pltpu.VMEM((TILES, 32, 128), F32),

time: 65.2 us -> 62.6 us (0.960)
  Pallas kernels: 62.7 us -> 60.1 us
    pallas_call x1, Pallas kernels: 62.7 us -> 60.1 us  [per_device(): pl.pallas_call(kernel, out_shape=(jax.ShapeDtypeStruct((1, 1, 1, ATOMS),...]
where the time goes in v3:
time: 62.6 us; the launch traced here: 62.5 us
  Pallas kernels  60.1 us (96%)
  other arithmetic  1.08 us (2%)
  between operations  0.66 us (1%)
    pallas_call x1, Pallas kernels, per_device(): pl.pallas_call(kernel, out_shape=(jax.ShapeDtypeStruct((1, 1, 1, ATOMS),...  60.1 us

profile of v3, /device:TPU:1, one launch (start us, length us, event | category | flops | bytes accessed | tf_op | source)
XLA Modules:
  0.0 62.5 jit_solution(7082635831761222362)
XLA Ops:
  0.6 60.1 %energy_and_forces.1 = (f32[1,1,1,18]{3,2,1,0:T(1,128)}, f32[1,1,3,1,18]{4,3,2,1,0:T(1,128)}) custom-call(f32[1,1,3,1,18]{4,3,2,1,0:T(1,128)} %bitcast.10, s32[1,1,1,18]{3,2,1,0:T(1,128)} %species_hbm.1, s32[1,1,1,18]{3,2,1,0:T(1,128)} %send_hbm.1, s32[1,1,18,1,56]{4,3,2,1,0:T(1,128)} %bitcast.8, f32[89,128]{1,0:T(8,128)} %emb_hbm.1, f32[1,89]{1,0:T(1,128)} %bitcast.11, ...), custom_call_target="tpu_custom_call" | custom-call | tf_op jit(solution)/shard_map/energy_and_forces/pallas_call | solution.py:658
  60.8 0.0 copy-start.1
  60.8 0.0 copy-start
  60.8 0.6 copy-done.1
  61.4 0.5 neg.17
  61.9 0.0 copy-done
  61.9 0.6 negate_bitcast_fusion
Async XLA Ops:
  60.8 0.6 %copy-start.1 = (f32[1,1,1,18]{3,2,1,0:T(1,128)S(1)}, f32[1,1,1,18]{3,2,1,0:T(1,128)}, u32[]{:S(2)}) copy-start(f32[1,1,1,18]{3,2,1,0:T(1,128)} %get-tuple-element.4) | copy-start | bytes 220
  60.8 1.1 %copy-start = (f32[1,1,3,1,18]{4,3,2,1,0:T(1,128)S(1)}, f32[1,1,3,1,18]{4,3,2,1,0:T(1,128)}, u32[]{:S(2)}) copy-start(f32[1,1,3,1,18]{4,3,2,1,0:T(1,128)} %get-tuple-element.5) | copy-start | bytes 652

commit v4 on v3

--- a/solution.py
+++ b/solution.py
@@ -32,7 +32,6 @@
         key=lambda b: -sum(abs(o) * w for o, w in zip(OFFSETS[b], (2, 1, 4))),
     )
 )
-PLACES = (0, 1, 2, 3, 5, 6, 7, 8)
 NN = ((1,), (0,))
 NT = ((1,), (1,))
 TN = ((0,), (0,))
@@ -90,6 +89,13 @@
 
 def lanes(index):
     return pl.ds(pl.multiple_of(index * 128, 128), 128)
+
+
+def even_series(square, first):
+    total = jnp.zeros_like(square)
+    for n in range(7, 0, -1):
+        total = (total + 1.0) * square * (-1.0 / ((2 * n + first) * (2 * n + first - 1)))
+    return total + 1.0
 
 
 def column(row, rows):
@@ -156,6 +162,7 @@
     basis_ref,
     dbasis_ref,
     harm,
+    tall,
     edge_grad,
     radial,
     slope,
@@ -208,6 +215,11 @@
         copy.start()
 
     across = jnp.where(lax.rem(me[2], 4) < 2, -1, 1)
+    twin = 1 - 2 * lax.rem(me[1], 2)
+    off = -twin
+
+    def place_of(ox, oy):
+        return 3 * (ox + 1) + oy + 1
 
     def remote(phase, index, src, dst, offset):
         return pltpu.make_async_remote_copy(
@@ -298,7 +310,7 @@
     h_zero = dot(own_hot, embedding, NN, HIGHEST)
     isolated = jnp.sum(own_hot * table_emb[128:129], axis=1, keepdims=True)
     emb_source = dot_split(jnp.transpose(source_ref[0]), embedding, NT)
-    emb_source = jnp.concatenate(halves(emb_source), axis=0).astype(BF16)
+    emb_source = parted(emb_source, 1)
 
     rin_high, rin_low = halves(jnp.concatenate([rin_ref[0], rin_ref[1]], axis=1))
     rin_wide = jnp.concatenate(
@@ -369,9 +381,9 @@
     weight = math.sqrt(2.0 / CUTOFF) * inverse * usable
     weight_grad = weight * (envelope_grad - envelope * inverse)
     weight = weight * envelope
-    angle = distance * (math.pi / CUTOFF)
-    sine_one = jnp.sin(angle)
-    cosine_one = jnp.cos(angle)
+    angle = (scaled - 0.5) * math.pi
+    sine_one = even_series(angle * angle, 0)
+    cosine_one = -angle * even_series(angle * angle, 1)
     sine, cosine = sine_one, cosine_one
     sine_last, cosine_last = jnp.zeros_like(angle), jnp.ones_like(angle)
     for m in range(ORDERS):
@@ -393,6 +405,8 @@
         )
     ):
         harm[:, m, :] = value
+        for k in range(TILES):
+            tall[k, m] = jnp.broadcast_to(value[k : k + 1], (8, 128))
 
     basis = jnp.concatenate([basis_ref[k] for k in range(TILES)], axis=1)
 
@@ -423,13 +437,13 @@
                 terms = [radial[t, rows[q], tile] * src for q in range(3)]
                 term[t, rows[0], tile] = terms[1]
                 term[t, rows[1], tile] = terms[2]
-                ys = harm[k]
+                terms = [value.reshape(CHUNK // 8, 8, 128) for value in terms]
                 parts = [terms[0]]
-                parts += [terms[1] * ys[m : m + 1] for m in range(3)]
-                parts += [terms[2] * ys[m : m + 1] for m in range(3, 8)]
+                parts += [terms[1] * tall[k, m][None] for m in range(3)]
+                parts += [terms[2] * tall[k, m][None] for m in range(3, 8)]
                 sums = [p if s is None else s + p for s, p in zip(sums, parts)]
             for i in range(9):
-                acc[i, rows[0], :] = sums[i]
+                acc[i, rows[0], :] = sums[i].reshape(CHUNK, 128)
             return carry
 
         lax.fori_loop(0, CHANNELS // CHUNK, chunk, 0)
@@ -507,26 +521,37 @@
 
     radial[0] = radial_out(0, hidden)
     element = geo[3]
-    for k in range(TILES):
-        tile = slice(128 * k, 128 * k + 128)
-        hot = (row.astype(F32) == element[k : k + 1]).astype(F32).astype(BF16)
-        both = dot(emb_source, hot, NN)
-        source[0, :, tile] = both[0:128] + both[128:256]
+    number = row.astype(F32)
+    hots = [(number == element[k : k + 1]).astype(F32) for k in range(TILES)]
+    hots = jnp.concatenate(hots, axis=1).astype(BF16)
+    source[0] = dot(emb_source, jnp.concatenate([hots, hots], axis=0), NN)
     invariants, parts_one = interaction(0)
 
     mine[...] = (zero_source + apply(invariants, chain_wide, NN))[0:ATOMS]
 
-    def second(place, level):
-        offset = (place // 3 - 1, place % 3 - 1, level)
-        slot = 9 * (1 - level) + 8 - place
-        return remote(1, slot, mine, feat.at[1 - level, 8 - place], offset)
-
-    for place in range(9):
-        second(place, across).start()
-    for place in range(9):
-        second(place, -across).start()
-    for place in PLACES:
-        second(place, 0).start()
+    def second(ox, oy, level, src, offset):
+        place = place_of(ox, oy)
+        return remote(1, 9 * (1 + level) + place, src, feat.at[1 + level, place], offset)
+
+    def outward(dx, dy, level):
+        return second(-dx, -dy, -level, mine, (dx, dy, level))
+
+    def arrival(ox, oy, level):
+        return second(ox, oy, level, mine, (0, twin, 0))
+
+    def hand_on(ox, level):
+        return second(ox, off, level, feat.at[1 + level, place_of(ox, 0)], (0, twin, 0))
+
+    for level in (across, -across):
+        for dx in (-1, 1, 0):
+            outward(dx, 0, level).start()
+        for dx in (-1, 1, 0):
+            outward(dx, off, level).start()
+    outward(0, twin, 0).start()
+    for dx in (-1, 1):
+        outward(dx, 0, 0).start()
+    for dx in (-1, 1, 0):
+        outward(dx, off, 0).start()
     table[...] = jnp.zeros_like(table)
     table[1, 4 * ROWS : 4 * ROWS + ATOMS] = mine[...]
     h_one = h_zero + dot_split(invariants, mix_ref[0], NN)
@@ -539,17 +564,28 @@
         slope[0, 128 * q : 128 * q + 128] = steep[128 * q : 128 * q + 128] * source[0]
     slope[1] = radial_out(1, tilted)
 
-    def gather(level, places):
-        for place in places:
-            second(8 - place, -level).wait_recv()
-            table[1 + level, ROWS * place : ROWS * place + ATOMS] = feat[1 + level, place]
+    def relay(level, sides):
+        for ox in sides:
+            arrival(ox, 0, level).wait_recv()
+            hand_on(ox, level).start()
+
+    def gather(level):
+        for ox in range(-1, 2):
+            arrival(ox, off, level).wait_recv()
+            arrival(ox, twin, level).wait_recv()
+        for place in range(9):
+            if not (place == 4 and isinstance(level, int)):
+                table[1 + level, ROWS * place : ROWS * place + ATOMS] = feat[1 + level, place]
         turned = parted(jnp.transpose(table[1 + level]), 0)
         both = dot(turned, onehot[1 + level], NN)
         return both[0:128] + both[128:256]
 
-    source[1] = gather(0, PLACES)
-    source[1] = source[1] + gather(-across, range(9))
-    source[1] = source[1] + gather(across, range(9))
+    relay(0, (-1, 1))
+    relay(-across, range(-1, 2))
+    source[1] = gather(0)
+    relay(across, range(-1, 2))
+    source[1] = source[1] + gather(-across)
+    source[1] = source[1] + gather(across)
 
     invariants, parts_two = interaction(1)
     inner = read_one + apply(invariants, read_in, NN)
@@ -558,22 +594,36 @@
     interaction_back(apply(inner_grad, read_out, NN), parts_two)
     source_back()
 
-    def third(place, level):
-        offset = (place // 3 - 1, place % 3 - 1, level)
+    def third(ox, oy, level, offset):
+        place = place_of(ox, oy)
         slot = 9 * (1 + level) + place
         return remote(2, slot, feat_grad.at[1 + level, place], feat_back.at[1 + level, place], offset)
 
-    def scatter(level, places):
+    def scatter(level):
         both = dot(onehot[1 + level], source_grad[...], NT)
         both = both[:, 0:128] + both[:, 128:256]
         for place in range(9):
             feat_grad[1 + level, place] = both[ROWS * place : ROWS * place + ATOMS]
-        for place in places:
-            third(place, level).start()
-
-    scatter(across, range(9))
-    scatter(-across, range(9))
-    scatter(0, PLACES)
+        for ox in (-1, 1, 0):
+            third(ox, twin, level, (0, twin, 0)).start()
+        for ox in (-1, 1, 0):
+            third(ox, off, level, (ox, off, level)).start()
+
+    def combine(level, sides):
+        for ox in sides:
+            third(ox, off, level, (0, twin, 0)).wait_recv()
+            place = place_of(ox, 0)
+            feat_grad[1 + level, place] = (
+                feat_grad[1 + level, place] + feat_back[1 + level, place_of(ox, off)]
+            )
+            third(ox, 0, level, (ox, 0, level)).start()
+
+    scatter(across)
+    scatter(-across)
+    combine(across, (-1, 1, 0))
+    scatter(0)
+    combine(-across, (-1, 1, 0))
+    combine(0, (-1, 1))
     grad_two = dot_split(inner_grad, read_hidden, NN) + read_one_ref[...]
     grad_two = dot_split(grad_two, mix_ref[0], NT)
     edge_back(1)
@@ -582,11 +632,15 @@
     )
     energy = jnp.sum((isolated + learned) * unsend[0:ROWS], axis=0, keepdims=True)
     energy_ref[0, 0] = -energy[:, 0:ATOMS]
-    total = feat_grad[1, 4]
-    for level, places in ((0, PLACES), (across, range(9)), (-across, range(9))):
-        for place in places:
-            third(place, level).wait_recv()
-            total = total + feat_back[1 + level, place]
+    third(0, off, 0, (0, twin, 0)).wait_recv()
+    total = feat_grad[1, 4] + feat_back[1, place_of(0, off)]
+    for level in (0, across, -across):
+        for ox in range(-1, 2):
+            if not (ox == 0 and isinstance(level, int)):
+                third(ox, 0, level, (0, twin, 0)).wait_recv()
+                total = total + feat_back[1 + level, place_of(ox, 0)]
+            third(ox, twin, level, (0, twin, 0)).wait_recv()
+            total = total + feat_back[1 + level, place_of(ox, twin)]
     own_rows = slice(4 * ROWS, 4 * ROWS + ROWS)
     table[1, 4 * ROWS : 4 * ROWS + ATOMS] = total
     grad_one = grad_two + apply(table[1, own_rows], chain_deep, NT)
@@ -634,9 +688,11 @@
     for copy in first + fourth:
         copy.wait_send()
     for level in range(-1, 2):
-        for place in PLACES if level == 0 else range(9):
-            second(place, level).wait_send()
-            third(place, level).wait_send()
+        for ox in range(-1, 2):
+            for oy in range(-1, 2):
+                if (ox, oy, level) != (0, 0, 0):
+                    second(ox, oy, level, mine, (0, twin, 0)).wait_send()
+                    third(ox, oy, level, (0, twin, 0)).wait_send()
 
 
 def per_device(
@@ -697,6 +753,7 @@
             pltpu.VMEM((TILES, ORDERS, 128), F32),
             pltpu.VMEM((TILES, ORDERS, 128), F32),
             pltpu.VMEM((TILES, 8, 128), F32),
+            pltpu.VMEM((TILES, 8, 8, 128), F32),
             pltpu.VMEM((2, TILES, 16, 128), F32),
             pltpu.VMEM((2, 384, EDGES), F32),
             pltpu.VMEM((2, 384, EDGES), F32),

time: 62.6 us -> 59.7 us (0.954)
  Pallas kernels: 60.1 us -> 57.2 us
    pallas_call x1, Pallas kernels: 60.1 us -> 57.2 us  [per_device(): pl.pallas_call(kernel, out_shape=(jax.ShapeDtypeStruct((1, 1, 1, ATOMS),...]
where the time goes in v4:
time: 59.7 us; the launch traced here: 59.5 us
  Pallas kernels  57.2 us (96%)
  other arithmetic  1.08 us (2%)
  between operations  0.66 us (1%)
  local copies, waits for them, and re-layouts  0.62 us (1%)
    pallas_call x1, Pallas kernels, per_device(): pl.pallas_call(kernel, out_shape=(jax.ShapeDtypeStruct((1, 1, 1, ATOMS),...  57.2 us

profile of v4, /device:TPU:1, one launch (start us, length us, event | category | flops | bytes accessed | tf_op | source)
XLA Modules:
  0.0 59.5 jit_solution(9560556021884661725)
XLA Ops:
  0.6 57.2 %energy_and_forces.1 = (f32[1,1,1,18]{3,2,1,0:T(1,128)}, f32[1,1,3,1,18]{4,3,2,1,0:T(1,128)}) custom-call(f32[1,1,3,1,18]{4,3,2,1,0:T(1,128)} %bitcast.10, s32[1,1,1,18]{3,2,1,0:T(1,128)} %species_hbm.1, s32[1,1,1,18]{3,2,1,0:T(1,128)} %send_hbm.1, s32[1,1,18,1,56]{4,3,2,1,0:T(1,128)} %bitcast.8, f32[89,128]{1,0:T(8,128)} %emb_hbm.1, f32[1,89]{1,0:T(1,128)} %bitcast.11, ...), custom_call_target="tpu_custom_call" | custom-call | tf_op jit(solution)/shard_map/energy_and_forces/pallas_call | solution.py:714
  57.8 0.0 copy-start.1
  57.8 0.0 copy-start
  57.8 0.6 %copy-done.1 = f32[1,1,1,18]{3,2,1,0:T(1,128)S(1)} copy-done((f32[1,1,1,18]{3,2,1,0:T(1,128)S(1)}, f32[1,1,1,18]{3,2,1,0:T(1,128)}, u32[]{:S(2)}) %copy-start.1) | copy-done | bytes 96
  58.4 0.5 neg.17
  58.9 0.0 copy-done
  58.9 0.6 negate_bitcast_fusion
Async XLA Ops:
  57.8 0.6 %copy-start.1 = (f32[1,1,1,18]{3,2,1,0:T(1,128)S(1)}, f32[1,1,1,18]{3,2,1,0:T(1,128)}, u32[]{:S(2)}) copy-start(f32[1,1,1,18]{3,2,1,0:T(1,128)} %get-tuple-element.4) | copy-start | bytes 220
  57.8 1.1 %copy-start = (f32[1,1,3,1,18]{4,3,2,1,0:T(1,128)S(1)}, f32[1,1,3,1,18]{4,3,2,1,0:T(1,128)}, u32[]{:S(2)}) copy-start(f32[1,1,3,1,18]{4,3,2,1,0:T(1,128)} %get-tuple-element.5) | copy-start | bytes 652

commit v5 on v4

--- a/solution.py
+++ b/solution.py
@@ -248,8 +248,14 @@
     arrived[OWN] = packed(own)
     arrived[27:32] = jnp.zeros((5, 1, 128), F32)
     pl.semaphore_wait(barrier, 26)
+    ways = [(dx, dy, level) for level in (across, -across) for dx in (-1, 1, 0) for dy in (-1, 1, 0)]
+    ways += [(dx, dy, 0) for dx in (-1, 1, 0) for dy in (-1, 1, 0) if (dx, dy) != (0, 0)]
+
+    def slot_of(way):
+        return 9 * (way[0] + 1) + 3 * (way[1] + 1) + way[2] + 1
+
     first = [
-        remote(0, b, packet.at[0], arrived.at[b], minus(OFFSETS[b])) for b in OTHERS
+        remote(0, slot_of(minus(w)), packet.at[0], arrived.at[slot_of(minus(w))], w) for w in ways
     ]
     for copy in first:
         copy.start()
@@ -668,7 +674,7 @@
     for b in range(27):
         leaving[b] = rows[b : b + 1]
     fourth = [
-        remote(3, b, leaving.at[b], returned.at[b], OFFSETS[b]) for b in OTHERS
+        remote(3, slot_of(w), leaving.at[slot_of(w)], returned.at[slot_of(w)], w) for w in ways
     ]
     for copy in fourth:
         copy.start()

time: 59.7 us -> 59.6 us (level)
  no operation moved by 1% of the time
where the time goes in v5:
time: 59.6 us; the launch traced here: 59.4 us
  Pallas kernels  57 us (96%)
  other arithmetic  1.08 us (2%)
  between operations  0.66 us (1%)
  local copies, waits for them, and re-layouts  0.62 us (1%)
    pallas_call x1, Pallas kernels, per_device(): pl.pallas_call(kernel, out_shape=(jax.ShapeDtypeStruct((1, 1, 1, ATOMS),...  57 us

profile of v5, /device:TPU:1, one launch (start us, length us, event | category | flops | bytes accessed | tf_op | source)
XLA Modules:
  0.0 59.4 jit_solution(16675211393139342599)
XLA Ops:
  0.6 57.0 %energy_and_forces.1 = (f32[1,1,1,18]{3,2,1,0:T(1,128)}, f32[1,1,3,1,18]{4,3,2,1,0:T(1,128)}) custom-call(f32[1,1,3,1,18]{4,3,2,1,0:T(1,128)} %bitcast.10, s32[1,1,1,18]{3,2,1,0:T(1,128)} %species_hbm.1, s32[1,1,1,18]{3,2,1,0:T(1,128)} %send_hbm.1, s32[1,1,18,1,56]{4,3,2,1,0:T(1,128)} %bitcast.8, f32[89,128]{1,0:T(8,128)} %emb_hbm.1, f32[1,89]{1,0:T(1,128)} %bitcast.11, ...), custom_call_target="tpu_custom_call" | custom-call | tf_op jit(solution)/shard_map/energy_and_forces/pallas_call | solution.py:720
  57.7 0.0 copy-start.1
  57.7 0.0 copy-start
  57.7 0.6 %copy-done.1 = f32[1,1,1,18]{3,2,1,0:T(1,128)S(1)} copy-done((f32[1,1,1,18]{3,2,1,0:T(1,128)S(1)}, f32[1,1,1,18]{3,2,1,0:T(1,128)}, u32[]{:S(2)}) %copy-start.1) | copy-done | bytes 96
  58.3 0.5 neg.17
  58.8 0.0 copy-done
  58.8 0.6 negate_bitcast_fusion
Async XLA Ops:
  57.7 0.6 %copy-start.1 = (f32[1,1,1,18]{3,2,1,0:T(1,128)S(1)}, f32[1,1,1,18]{3,2,1,0:T(1,128)}, u32[]{:S(2)}) copy-start(f32[1,1,1,18]{3,2,1,0:T(1,128)} %get-tuple-element.4) | copy-start | bytes 220
  57.7 1.1 %copy-start = (f32[1,1,3,1,18]{4,3,2,1,0:T(1,128)S(1)}, f32[1,1,3,1,18]{4,3,2,1,0:T(1,128)}, u32[]{:S(2)}) copy-start(f32[1,1,3,1,18]{4,3,2,1,0:T(1,128)} %get-tuple-element.5) | copy-start | bytes 652
